TPU v7x, 256 devices: a whole 4x4x8 slice. The times are simulated.
256 devices in a mesh: blk: 16 (over y_lo, z), tp: 4 (over y_hi, core), dp: 4 (over x).
Axes of the slice: x: 4, y: 4 (y_hi: 2, y_lo: 2; y = y_hi * 2 + y_lo), z: 8, core: 2. Of those that a mesh axis runs over, the one named last changes fastest.
Arguments:
- layer_input: bfloat16 [24576, 8192], P(('blk', 'dp')), may hold values from -16 to 16
- queries: bfloat16 [24576, 4096], P(('blk', 'dp'), 'tp'), may hold values from -160 to 160
- keys: bfloat16 [24576, 512], P(('blk', 'dp'), 'tp'), may hold values from -7 to 7
- values: bfloat16 [24576, 512], P(('blk', 'dp'), 'tp'), may hold values from -6 to 6
- kv_weight: bfloat16 [8192, 1024], P('blk', 'tp'), may hold values from -0.0625 to 0.0625
- out_grad: bfloat16 [24576, 4096], P(('blk', 'dp'), 'tp'), may hold values from -6 to 6
- doc_lengths: int32 [64, 4], P(('blk', 'dp')), may hold values from 1 to 192, 384 in all within a row
Outputs:
- input_grad: bfloat16 [24576, 8192], P(('blk', 'dp'), 'tp')
- query_grad: bfloat16 [24576, 4096], P(('blk', 'dp'), 'tp')
- weight_grad: float32 [8192, 1024], P('blk', 'tp')
All inputs are finite; a program needn't handle non-finite values.
Results may differ from a plain program's by a relative error of at most 0.015.
Values may be sent and summed in bfloat16 or wider, within the bound.
A program may use at most 128 MiB of HBM per device.

v0:
```python
import jax
import jax.numpy as jnp
from jax import lax
from jax.sharding import PartitionSpec as P

HD = 128


def attend_back(queries, keys, values, out_grad, lengths):
    tokens_here = queries.shape[0]
    local_kv = keys.shape[1] // HD
    group_size = queries.shape[1] // keys.shape[1]
    query_heads = queries.reshape(tokens_here, local_kv, group_size, HD)
    key_heads = keys.reshape(tokens_here, local_kv, HD)
    value_heads = values.reshape(tokens_here, local_kv, HD)
    grad_heads = out_grad.reshape(tokens_here, local_kv, group_size, HD)
    positions = jnp.arange(tokens_here, dtype=jnp.int32)
    doc_ends = jnp.cumsum(lengths)
    documents = jnp.sum((positions[:, None] >= doc_ends[None, :]).astype(jnp.int32), axis=1)
    allowed = (documents[:, None] == documents[None, :]) & (
        positions[None, :] <= positions[:, None]
    )
    score_scale = 1.0 / HD**0.5
    scores = (
        jnp.einsum("ikgd,jkd->kgij", query_heads, key_heads, preferred_element_type=jnp.float32)
        * score_scale
    )
    scores = jnp.where(allowed[None, None], scores, -1e30)
    peaks = jnp.max(scores, axis=-1, keepdims=True)
    powers = jnp.exp(scores - peaks)
    soft_probs = powers / jnp.sum(powers, axis=-1, keepdims=True)
    probs_low = soft_probs.astype(jnp.bfloat16)
    prob_grad = jnp.einsum(
        "ikgd,jkd->kgij", grad_heads, value_heads, preferred_element_type=jnp.float32
    )
    inner = jnp.sum(soft_probs * prob_grad, axis=-1, keepdims=True)
    score_grad = (soft_probs * (prob_grad - inner) * score_scale).astype(jnp.bfloat16)
    query_grad = jnp.einsum(
        "kgij,jkd->ikgd", score_grad, key_heads, preferred_element_type=jnp.float32
    ).astype(jnp.bfloat16)
    key_grad = jnp.einsum(
        "kgij,ikgd->jkd", score_grad, query_heads, preferred_element_type=jnp.float32
    )
    value_grad = jnp.einsum(
        "kgij,ikgd->jkd", probs_low, grad_heads, preferred_element_type=jnp.float32
    )
    kv_grad = jnp.stack([key_grad, value_grad], axis=2).astype(jnp.bfloat16)
    return (
        query_grad.reshape(tokens_here, queries.shape[1]),
        kv_grad.reshape(tokens_here, local_kv * 2 * HD),
    )


def shards(layer_input, queries, keys, values, kv_weight, out_grad, doc_lengths):
    query_grad, kv_grad = attend_back(queries, keys, values, out_grad, doc_lengths[0])
    partial_grad = lax.dot_general(
        kv_grad,
        lax.all_gather(kv_weight, "blk", axis=0, tiled=True),
        (((1,), (1,)), ((), ())),
        preferred_element_type=jnp.float32,
    )
    input_grad = lax.psum_scatter(partial_grad, "tp", scatter_dimension=1, tiled=True).astype(
        jnp.bfloat16
    )
    owner_rows = lax.psum_scatter(
        lax.dot_general(
            layer_input, kv_grad, (((0,), (0,)), ((), ())), preferred_element_type=jnp.float32
        ),
        "blk",
        scatter_dimension=0,
        tiled=True,
    )
    weight_grad = lax.psum(owner_rows, "dp")
    return (input_grad, query_grad, weight_grad)


def solution(mesh):
    placed = (
        P(("blk", "dp"), None),
        P(("blk", "dp"), "tp"),
        P(("blk", "dp"), "tp"),
        P(("blk", "dp"), "tp"),
        P("blk", "tp"),
        P(("blk", "dp"), "tp"),
        P(("blk", "dp"), None),
    )
    return jax.shard_map(
        shards,
        mesh=mesh,
        in_specs=placed,
        out_specs=(P(("blk", "dp"), "tp"), P(("blk", "dp"), "tp"), P("blk", "tp")),
        check_vma=False,
    )
```

profile of v0, /device:TPU:2, one launch (start us, length us, event | category | flops | bytes accessed | tf_op | source)
XLA Modules:
  0.0 377.2 jit_solution(14370500028808519840)
XLA Ops:
  7.2 0.0 copy-start
  7.2 0.0 reduce-scatter.5.cloned.1.call-start
  7.2 0.8 reduce-window.8
  8.1 0.1 convert_reduce_fusion
  8.1 0.1 fusion.23
  8.3 1.5 copy.35
  9.8 1.5 copy.36
  11.3 0.9 fusion.6
  12.2 1.0 fusion.5
  13.2 0.0 slice-start
  13.2 1.4 fusion.20
  14.6 0.0 slice-start.1
  14.6 1.6 fusion
  16.3 1.6 fusion.7
  17.9 0.8 fusion.19
  18.8 5.6 %convolution_bitcast_fusion = f32[8192,256]{0,1:T(8,128)} fusion(bf16[384,256]{0,1:T(8,128)(2,1)S(1)} %bitcast.119, bf16[384,8192]{1,0:T(8,128)(2,1)S(1)} %bitcast.115), kind=kOutput, calls=%fused_computation | convolution fusion | flops 1610612736 | bytes 14876672 | tf_op jit(solution)/shard_map/dot_general | solution.py:66
  24.4 0.0 reduce-scatter.5.cloned.1.call-update
  24.4 0.0 all-gather.2.cloned.1.call-start
  24.4 0.7 all-gather.2.cloned.1.call-update
  25.1 0.0 all-reduce.2.cloned.1.call-start
  25.2 103.5 %reduce-scatter.5.cloned.1.call-done = f32[512,256]{0,1:T(8,128)} async-done(((f32[8192,256]{0,1:T(8,128)}), f32[512,256]{0,1:T(8,128)}) %reduce-scatter.5.cloned.1.call-update) | async-done | bytes 524304 | tf_op jit(solution)/shard_map/reduce_scatter | solution.py:65
  128.6 0.0 all-reduce.2.cloned.1.call-update
  128.7 0.2 reduce-scatter.3.cloned.1.call-start
  128.9 76.1 %all-gather.2.cloned.1.call-done = bf16[8192,256]{1,0:T(8,128)(2,1)} async-done(((bf16[512,256]{1,0:T(8,128)(2,1)}), bf16[8192,256]{1,0:T(8,128)(2,1)}) %all-gather.2.cloned.1.call-update) | async-done | bytes 4194320 | tf_op jit(solution)/shard_map/all_gather | solution.py:58
  205.0 8.6 %fusion.31 = f32[384,8192]{1,0:T(8,128)} fusion(bf16[384,256]{0,1:T(8,128)(2,1)S(1)} %bitcast.120, bf16[8192,256]{1,0:T(8,128)(2,1)} %all-gather.2.cloned.1.call-done), kind=kOutput, calls=%fused_computation.35 | convolution fusion | flops 1610612736 | bytes 16973824 | tf_op jit(solution)/shard_map/dot_general | solution.py:56
  213.6 0.0 reduce-scatter.3.cloned.1.call-update
  213.7 0.6 convolution_convert_fusion
  214.3 1.2 copy.28
  215.5 36.5 %all-reduce.2.cloned.1.call-done = f32[512,256]{0,1:T(8,128)} async-done(((f32[512,256]{0,1:T(8,128)}), f32[512,256]{0,1:T(8,128)}) %all-reduce.2.cloned.1.call-update) | async-done | bytes 524304 | tf_op jit(solution)/shard_map/psum | solution.py:73
  251.9 2.0 copy.29
  254.0 113.5 %reduce-scatter.3.cloned.1.call-done = f32[384,2048]{1,0:T(8,128)} async-done(((f32[384,8192]{1,0:T(8,128)}), f32[384,2048]{1,0:T(8,128)}) %reduce-scatter.3.cloned.1.call-update) | async-done | bytes 3145744 | tf_op jit(solution)/shard_map/reduce_scatter | solution.py:62
  367.4 3.3 convert_element_type.35
  (7 shorter events, 0.0 us)
Async XLA Ops:
  7.2 4.1 %copy-start = (bf16[384,128]{1,0:T(8,128)(2,1)S(1)}, bf16[384,128]{1,0:T(8,128)(2,1)}, u32[]{:S(2)}) copy-start(bf16[384,128]{1,0:T(8,128)(2,1)} %param.9) | copy-start | bytes 294916
  7.2 121.5 %reduce-scatter.5.cloned.1.call-start = ((), (), s32[]{:S(2)}) async-start(), calls=%async_computation.4 | async-start | bytes 8912896 | tf_op jit(solution)/shard_map/reduce_scatter | solution.py:65
  13.1 1.5 copy-start.1
  13.2 5.6 %slice-start = ((s8[6291456]{0:T(1024)(128)(4,1)}), s8[4194304]{0:T(1024)(128)(4,1)S(1)}, s32[]{:S(2)}) async-start(s8[6291456]{0:T(1024)(128)(4,1)} %bitcast.114), calls=%async_computation.6 | async-start | bytes 8388608
  14.6 4.1 %slice-start.1 = ((s8[6291456]{0:T(1024)(128)(4,1)}), s8[2097152]{0:T(1024)(128)(4,1)S(1)}, s32[]{:S(2)}) async-start(s8[6291456]{0:T(1024)(128)(4,1)} %bitcast.114), calls=%async_computation.7 | async-start | bytes 4194304
  24.4 180.6 %all-gather.2.cloned.1.call-start = ((), (), s32[]{:S(2)}) async-start(), calls=%async_computation.2 | async-start | bytes 4456448 | tf_op jit(solution)/shard_map/all_gather | solution.py:58
  25.1 226.8 %all-reduce.2.cloned.1.call-start = ((), (), s32[]{:S(2)}) async-start(), calls=%async_computation.5 | async-start | bytes 1048576 | tf_op jit(solution)/shard_map/psum | solution.py:73
  128.7 238.8 %reduce-scatter.3.cloned.1.call-start = ((), (), s32[]{:S(2)}) async-start(), calls=%async_computation.3 | async-start | bytes 15728640 | tf_op jit(solution)/shard_map/reduce_scatter | solution.py:62
Sparse Core Ops, SparseCore 0:
  24.5 104.0 reduce-scatter.4
  130.4 74.5 all-gather.1
  207.4 44.5 all-reduce.1
  254.6 112.7 reduce-scatter.2
where the time goes:
time: 378 us; the launch traced here: 377 us
  waiting for transfers between devices  330 us (87%)
  matrix products  19.6 us (5%)
  between operations  13.9 us (4%)
  other arithmetic  6.92 us (2%)
  local copies, waits for them, and re-layouts  6.21 us (2%)
    reduce_scatter x1, waiting for transfers between devices, shards(): lax.psum_scatter(partial_grad, 'tp', scatter_dimension=1, tiled=True)  113 us
    reduce_scatter x1, waiting for transfers between devices, shards(): lax.psum_scatter(lax.dot_general(layer_input, kv_grad, (((0,), (0,)), (()...  103 us
    all_gather x1, waiting for transfers between devices, shards(): lax.all_gather(kv_weight, 'blk', axis=0, tiled=True)  76.1 us
    psum x1, waiting for transfers between devices, shards(): weight_grad = lax.psum(owner_rows, 'dp')  36.5 us
    dot_general x1, matrix products, shards(): lax.dot_general(kv_grad, lax.all_gather(kv_weight, 'blk', axis=0, tiled=T...  8.62 us
  transfers between devices with their start and end apart: 4, of which 4 were waited for; matrix products, arithmetic and copies ran while one was open for 3% of the time, Pallas kernels for 0%

commit v1 on v0

v1 whole, which is shorter than its diff:
```python
import functools

import jax
import jax.numpy as jnp
from jax import lax
from jax.experimental import pallas as pl
from jax.experimental.pallas import tpu as pltpu
from jax.sharding import PartitionSpec as P

HD = 128
MESH = pl.DeviceIdType.MESH
F32 = jnp.float32
BF16 = jnp.bfloat16


def device(x, y, z, c):
    return {"blk": (y % 2) * 8 + z, "tp": (y // 2) * 2 + c, "dp": x}


def dot(a, b, dims):
    return lax.dot_general(a, b, (dims, ((), ())), preferred_element_type=F32)


def kernel(
    li, q, k, v, w, do, dl,
    ig, qg, wg,
    xb, wz, wfull, kv_all, kv_oth, kvt, sbuf, rbuf, facc, xs, xr, fin, wgt, bias, kacc, vacc,
    xo_sem, xs_s, xs_r, xsib_s, xsib_r,
    w0_s, w0_r, wz_s, wz_r, wx_s, wx_r, wsib_s, wsib_r, wloc,
    k1_s, k1_r, k2_s, k2_r, ks_s, ks_r,
    rs_s, rs_r, xr_s, xr_r, fin_s, fin_r,
):
    blk, tp, x = lax.axis_index("blk"), lax.axis_index("tp"), lax.axis_index("dp")
    yl, z, yh, c = blk // 8, blk % 8, tp // 2, tp % 2
    y = yh * 2 + yl
    p = x % 2

    def remote(src, dst, ssem, rsem, dev):
        return pltpu.make_async_remote_copy(
            src_ref=src, dst_ref=dst, send_sem=ssem, recv_sem=rsem,
            device_id=dev, device_id_type=MESH,
        )

    def at(dx=0, dy=0, dz=0, core=None):
        return device((x + dx) % 4, (y + dy) % 4, (z + dz) % 8, c if core is None else core)

    sibling = at(core=1 - c)

    partners = [at(dz=1), at(dz=7), sibling, at(dy=1), at(dy=2), at(dy=3), at(dx=2)]
    for dx in (1, 3):
        for core in (0, 1):
            partners.append(at(dx=dx, core=core))
    for dx in (1, 2, 3):
        for dy in (1, 3):
            partners.append(at(dx=dx, dy=dy))
    barrier = pltpu.get_barrier_semaphore()
    for d in partners:
        pl.semaphore_signal(barrier, inc=1, device_id=d, device_id_type=MESH)

    def x_own(zp):
        cols = pl.ds(pl.multiple_of(((1 - yl) * 8 + zp) * 512 + yh * 256, 256), 256)
        return pltpu.make_async_copy(li.at[:, cols], xb.at[zp, pl.ds(0, 384)], xo_sem.at[zp])

    for zp in range(8):
        x_own(zp).start()

    pl.semaphore_wait(barrier, len(partners))

    rows_p = pl.ds(pl.multiple_of(p * 256, 256), 256)

    def w0_remote(i):
        return remote(
            w.at[rows_p], wz.at[z, yh], w0_s.at[i], w0_r.at[yh],
            device(x, 2 * yl + i, z, c),
        )

    def w0_local(i):
        return pltpu.make_async_copy(w.at[rows_p], wz.at[z, yh], w0_r.at[yh])

    for i in range(2):
        @pl.when(2 * yl + i != y)
        def _():
            w0_remote(i).start()

        @pl.when(2 * yl + i == y)
        def _():
            w0_local(i).start()

    def x_send(side, j):
        ydst = (y + 1) % 4 if side == 0 else (y + 3) % 4
        zp = 4 * c + j
        cols = pl.ds(pl.multiple_of((yl * 8 + zp) * 512 + (ydst // 2) * 256, 256), 256)
        return remote(
            li.at[pl.ds(192 * side, 192), cols],
            xb.at[zp, pl.ds(384 + 192 * side, 192)],
            xs_s.at[side, j], xs_r.at[side, j], device(x, ydst, z, c),
        )

    for j in range(4):
        for side in range(2):
            x_send(side, j).start()

    def x_relay():
        mine = pl.ds(4 * c, 4)
        return remote(
            xb.at[mine, pl.ds(384, 384)], xb.at[mine, pl.ds(384, 384)],
            xsib_s, xsib_r, sibling,
        )

    def spread_x(zp, side):
        j, cz = zp % 4, zp // 4
        return remote(
            wz.at[zp, side], wfull.at[j, c, side, rows_p],
            wx_s.at[zp, side], wx_r.at[j, c, side],
            at(dx=1 if side == 0 else 3, core=cz),
        )

    def spread_sibling(zp):
        j = zp % 4
        return remote(
            wz.at[zp], wfull.at[j, c, :, rows_p], wsib_s.at[zp], wsib_r.at[j], sibling
        )

    def spread_local(zp):
        j = zp % 4
        return pltpu.make_async_copy(wz.at[zp], wfull.at[j, c, :, rows_p], wloc.at[j])

    def spread(zp):
        for side in range(2):
            spread_x(zp, side).start()

        @pl.when(zp // 4 == c)
        def _():
            spread_local(zp).start()

        @pl.when(zp // 4 != c)
        def _():
            spread_sibling(zp).start()

    def wz_copy(direction, s):
        zp = (z - s + 8) % 8 if direction == 0 else (z + s) % 8
        ref = wz.at[zp, direction] if s == 3 else wz.at[zp]
        return remote(
            ref, ref, wz_s.at[direction, s], wz_r.at[direction, s],
            at(dz=1 if direction == 0 else 7),
        )

    def wz_wait(direction, s):
        zp = (z - s + 7) % 8 if direction == 0 else (z + s + 1) % 8
        ref = wz.at[zp, direction] if s == 3 else wz.at[zp]
        remote(ref, ref, wz_s.at[direction, s], wz_r.at[direction, s], sibling).wait_recv()
        return zp

    def w_begin():
        for h in range(2):
            remote(w.at[rows_p], wz.at[z, h], w0_s.at[h], w0_r.at[h], sibling).wait_recv()
        for direction in range(2):
            wz_copy(direction, 0).start()
        spread(z)

    def w_step(s):
        arrived = [wz_wait(direction, s) for direction in range(2)]
        if s < 3:
            for direction in range(2):
                wz_copy(direction, s + 1).start()
            for zp in arrived:
                spread(zp)
        else:
            spread(arrived[0])

    lens = [dl[0, i] for i in range(3)]
    ends = [lens[0], lens[0] + lens[1], lens[0] + lens[1] + lens[2]]

    def documents(shape, dim):
        pos = lax.broadcasted_iota(jnp.int32, shape, dim)
        return pos, sum((pos >= e).astype(jnp.int32) for e in ends)

    kpos, kdoc = documents((384, 1), 0)
    qpos, qdoc = documents((1, 384), 1)
    bias[...] = jnp.where((kdoc == qdoc) & (kpos <= qpos), 0.0, -1e30).astype(F32)
    kacc[...] = jnp.zeros_like(kacc)
    vacc[...] = jnp.zeros_like(vacc)
    scale = 1.0 / HD**0.5

    def head(h, carry):
        lanes = pl.ds(pl.multiple_of(h * HD, HD), HD)
        for b in range(3):
            n = 128 * (b + 1)
            rows = pl.ds(128 * b, 128)
            qb, gb = q[rows, lanes], do[rows, lanes]
            s = dot(k[:n], qb, ((1,), (1,))) + bias[:n, 128 * b:n]
            e = jnp.exp((s - jnp.max(s, axis=0, keepdims=True)) * scale)
            probs = e * (1.0 / jnp.sum(e, axis=0, keepdims=True))
            pg = dot(v[:n], gb, ((1,), (1,)))
            inner = jnp.sum(probs * pg, axis=0, keepdims=True)
            ds = (probs * (pg - inner) * scale).astype(BF16)
            qg[rows, lanes] = dot(ds, k[:n], ((0,), (0,))).astype(BF16)
            kacc[:n] += dot(ds, qb, ((1,), (0,)))
            vacc[:n] += dot(probs.astype(BF16), gb, ((1,), (0,)))
        return carry

    lax.fori_loop(0, 2, head, 0)
    w_begin()
    lax.fori_loop(2, 8, head, 0)

    kv_all[c, yh, :, :HD] = kacc[...].astype(BF16)
    kv_all[c, yh, :, HD:] = vacc[...].astype(BF16)

    def kv1(side):
        return remote(
            kv_all.at[c, yh], kv_oth.at[yh], k1_s.at[side], k1_r.at[yh],
            at(dy=1 if side == 0 else 3),
        )

    for side in range(2):
        kv1(side).start()

    def kv_sibling(i):
        ref = kv_all.at[c, yh] if i == 0 else kv_all.at[c, 1 - yh]
        return remote(ref, ref, ks_s.at[i], ks_r.at[i], sibling)

    kv_sibling(0).start()

    def kv2(side):
        hsrc = ((y + 3) % 4) // 2 if side == 0 else ((y + 1) % 4) // 2
        rows = pl.ds(192 * side, 192)
        return remote(
            kv_oth.at[hsrc, rows], kv_all.at[c, hsrc, rows], k2_s.at[side], k2_r.at[side],
            at(dy=1 if side == 0 else 3),
        )

    def transpose_kv(h):
        kvt[h, :, :384] = kv_all[c, h].astype(F32).T.astype(BF16)
        kvt[h, :, 384:] = kv_oth[h].astype(F32).T.astype(BF16)

    def partial(h, zp, rows=slice(None)):
        return dot(kvt[h, rows, :], xb[zp], ((1,), (0,)))

    def rs_copy(f, direction, s):
        half = pl.ds(0, 128) if s == 0 else pl.ds(0, 256)
        return remote(
            sbuf.at[f, direction, s, half], rbuf.at[f, direction, s, half],
            rs_s.at[f, direction, s], rs_r.at[f, direction, s],
            at(dz=1 if direction == 0 else 7),
        )

    def rs_step(f, s):
        h = yh if f == 0 else 1 - yh
        terms = []
        for direction in range(2):
            zd = (z + 4 - s) % 8 if direction == 0 else (z + 4 + s) % 8
            if s == 0:
                terms.append(partial(h, zd, slice(128 * direction, 128 * direction + 128)))
            else:
                terms.append(partial(h, zd))
        for direction in range(2):
            if s == 0:
                sbuf[f, direction, 0, :128] = terms[direction].astype(BF16)
            else:
                rs_copy(f, direction, s - 1).wait_recv()
                if s == 1:
                    mine = slice(128 * direction, 128 * direction + 128)
                    rest = slice(128 - 128 * direction, 256 - 128 * direction)
                    sbuf[f, direction, 1, rest] = terms[direction][rest].astype(BF16)
                    sbuf[f, direction, 1, mine] = (
                        terms[direction][mine] + rbuf[f, direction, 0, :128].astype(F32)
                    ).astype(BF16)
                else:
                    sbuf[f, direction, s] = (
                        terms[direction] + rbuf[f, direction, s - 1].astype(F32)
                    ).astype(BF16)
            rs_copy(f, direction, s).start()

    def x_copy(f, i):
        quarter = pl.ds(pl.multiple_of(((x + i) % 4) * 64, 64), 64)
        return remote(
            xs.at[f, quarter], xr.at[f, i - 1], xr_s.at[f, i - 1], xr_r.at[f, i - 1], at(dx=i)
        )

    def rs_last(f):
        h = yh if f == 0 else 1 - yh
        total = partial(h, z)
        for direction in range(2):
            rs_copy(f, direction, 3).wait_recv()
            total = total + rbuf[f, direction, 3].astype(F32)
        facc[f] = total
        xs[f] = total.astype(BF16)
        for i in (2, 1, 3):
            x_copy(f, i).start()

    def fin_copy(f, i):
        h = yh if f == 0 else 1 - yh
        cols = pl.ds(pl.multiple_of(x * 64, 64), 64)
        return remote(
            fin.at[f], wgt.at[yh, cols], fin_s.at[f, i], fin_r.at[yh, x],
            device((x + i) % 4, 2 * h + 1 - yl, z, c),
        )

    def x_last(f):
        total = facc[f, pl.ds(pl.multiple_of(x * 64, 64), 64)]
        for i in range(1, 4):
            x_copy(f, i).wait_recv()
            total = total + xr[f, i - 1].astype(F32)
        fin[f] = total.astype(BF16)
        for i in (2, 1, 3, 0):
            fin_copy(f, i).start()

    for j in range(4):
        for side in range(2):
            x_send(side, j).wait_recv()
    x_relay().start()
    w_step(0)
    for zp in range(8):
        x_own(zp).wait()

    for h in range(2):
        remote(
            kv_all.at[c, yh], kv_oth.at[h], k1_s.at[h], k1_r.at[h], sibling
        ).wait_recv()
    for side in range(2):
        kv2(side).start()
    transpose_kv(yh)
    theirs = pl.ds(4 * (1 - c), 4)
    remote(
        xb.at[theirs, pl.ds(384, 384)], xb.at[theirs, pl.ds(384, 384)], xsib_s, xsib_r, sibling
    ).wait_recv()
    rs_step(0, 0)
    w_step(1)
    rs_step(0, 1)
    for side in range(2):
        rows = pl.ds(192 * side, 192)
        remote(
            kv_oth.at[0, rows], kv_all.at[c, 1 - yh, rows], k2_s.at[side], k2_r.at[side], sibling
        ).wait_recv()
    kv_sibling(1).start()
    transpose_kv(1 - yh)
    rs_step(1, 0)
    w_step(2)
    rs_step(0, 2)
    rs_step(1, 1)
    rs_step(0, 3)
    rs_step(1, 2)
    w_step(3)
    rs_last(0)
    rs_step(1, 3)
    x_last(0)
    rs_last(1)

    for i in range(2):
        ref = kv_all.at[1 - c, yh] if i == 0 else kv_all.at[1 - c, 1 - yh]
        remote(ref, ref, ks_s.at[i], ks_r.at[i], sibling).wait_recv()

    def w_ready(j):
        pltpu.make_async_copy(wz.at[0], wfull.at[j, c, :, rows_p], wloc.at[j]).wait()
        remote(
            wz.at[0], wfull.at[j, 1 - c, :, rows_p], wsib_s.at[0], wsib_r.at[j], sibling
        ).wait_recv()
        rows_o = pl.ds(pl.multiple_of((1 - p) * 256, 256), 256)
        for cc in range(2):
            for side in range(2):
                remote(
                    wz.at[0, side], wfull.at[j, cc, side, rows_o],
                    wx_s.at[0, side], wx_r.at[j, cc, side], sibling,
                ).wait_recv()

    def ig_step(j):
        w_ready(j)
        total = None
        for cc in range(2):
            for h in range(2):
                term = dot(kv_all[cc, h], wfull[j, cc, h], ((1,), (1,)))
                total = term if total is None else total + term
        ig[:, 512 * j:512 * j + 512] = total.astype(BF16)

    ig_step(0)
    ig_step(1)
    x_last(1)
    ig_step(2)
    ig_step(3)

    for hs in range(2):
        for xx in range(4):
            remote(
                fin.at[0], wgt.at[hs, pl.ds(64 * xx, 64)], fin_s.at[0, 0], fin_r.at[hs, xx], sibling
            ).wait_recv()
        wg[256 * hs:256 * hs + 256, :] = wgt[hs].astype(F32).T

    for i in range(2):
        @pl.when(2 * yl + i != y)
        def _():
            w0_remote(i).wait_send()
    for side in range(2):
        for j in range(4):
            x_send(side, j).wait_send()
        kv1(side).wait_send()
        kv2(side).wait_send()
        kv_sibling(side).wait_send()
        for s in range(4):
            wz_copy(side, s).wait_send()
            for f in range(2):
                rs_copy(f, side, s).wait_send()
    x_relay().wait_send()
    for zp in range(8):
        for side in range(2):
            spread_x(zp, side).wait_send()

        @pl.when(zp // 4 != c)
        def _():
            spread_sibling(zp).wait_send()
    for f in range(2):
        for i in range(1, 4):
            x_copy(f, i).wait_send()
        for i in range(4):
            fin_copy(f, i).wait_send()


def shards(layer_input, queries, keys, values, kv_weight, out_grad, doc_lengths):
    vmem = pl.BlockSpec(memory_space=pltpu.VMEM)
    hbm = pl.BlockSpec(memory_space=pl.ANY)
    smem = pl.BlockSpec(memory_space=pltpu.SMEM)
    dma = pltpu.SemaphoreType.DMA
    return pl.pallas_call(
        kernel,
        out_shape=(
            jax.ShapeDtypeStruct((384, 2048), BF16),
            jax.ShapeDtypeStruct((384, 1024), BF16),
            jax.ShapeDtypeStruct((512, 256), F32),
        ),
        in_specs=[hbm, vmem, vmem, vmem, vmem, vmem, smem],
        out_specs=(vmem, vmem, vmem),
        scratch_shapes=[
            pltpu.VMEM((8, 768, 256), BF16),
            pltpu.VMEM((8, 2, 256, 256), BF16),
            pltpu.VMEM((4, 2, 2, 512, 256), BF16),
            pltpu.VMEM((2, 2, 384, 256), BF16),
            pltpu.VMEM((2, 384, 256), BF16),
            pltpu.VMEM((2, 256, 768), BF16),
            pltpu.VMEM((2, 2, 4, 256, 256), BF16),
            pltpu.VMEM((2, 2, 4, 256, 256), BF16),
            pltpu.VMEM((2, 256, 256), F32),
            pltpu.VMEM((2, 256, 256), BF16),
            pltpu.VMEM((2, 3, 64, 256), BF16),
            pltpu.VMEM((2, 64, 256), BF16),
            pltpu.VMEM((2, 256, 256), BF16),
            pltpu.VMEM((384, 384), F32),
            pltpu.VMEM((384, 128), F32),
            pltpu.VMEM((384, 128), F32),
            dma((8,)), dma((2, 4)), dma((2, 4)), dma, dma,
            dma((2,)), dma((2,)), dma((2, 4)), dma((2, 4)),
            dma((8, 2)), dma((4, 2, 2)), dma((8,)), dma((4,)), dma((4,)),
            dma((2,)), dma((2,)), dma((2,)), dma((2,)), dma((2,)), dma((2,)),
            dma((2, 2, 4)), dma((2, 2, 4)), dma((2, 3)), dma((2, 3)),
            dma((2, 4)), dma((2, 4)),
        ],
        compiler_params=pltpu.CompilerParams(
            collective_id=0, has_side_effects=True, vmem_limit_bytes=56 << 20
        ),
        cost_estimate=pl.CostEstimate(
            flops=5 * 10**9, bytes_accessed=2 * 10**7, transcendentals=10**6
        ),
        name="kv_back",
    )(layer_input, queries, keys, values, kv_weight, out_grad, doc_lengths)


def solution(mesh):
    placed = (
        P(("blk", "dp"), None),
        P(("blk", "dp"), "tp"),
        P(("blk", "dp"), "tp"),
        P(("blk", "dp"), "tp"),
        P("blk", "tp"),
        P(("blk", "dp"), "tp"),
        P(("blk", "dp"), None),
    )
    return jax.shard_map(
        shards,
        mesh=mesh,
        in_specs=placed,
        out_specs=(P(("blk", "dp"), "tp"), P(("blk", "dp"), "tp"), P("blk", "tp")),
        check_vma=False,
    )
```

time: 378 us -> 81 us (0.21)
  waiting for transfers between devices: 330 us -> 0 us
  Pallas kernels: 0 us -> 74.4 us
  matrix products: 19.6 us -> 0 us
  between operations: 13.9 us -> 0.65 us
  other arithmetic: 6.92 us -> 0 us
    reduce_scatter x2 -> x0, waiting for transfers between devices: 217 us -> none  [the longest x1 113 us: shards(): lax.psum_scatter(partial_grad, 'tp', scatter_dimension=1, tiled=True)]
    all_gather x1 -> x0, waiting for transfers between devices: 76.1 us -> none  [shards(): lax.all_gather(kv_weight, 'blk', axis=0, tiled=True)]
    pallas_call x0 -> x1, Pallas kernels: none -> 74.4 us  [shards(): pl.pallas_call(kernel, out_shape=(jax.ShapeDtypeStruct((384, 2048), BF16)...]
    psum x1 -> x0, waiting for transfers between devices: 36.5 us -> none  [shards(): weight_grad = lax.psum(owner_rows, 'dp')]
    dot_general x7 -> x0, matrix products: 19.6 us -> none  [the longest x1 8.62 us: shards(): lax.dot_general(kv_grad, lax.all_gather(kv_weight, 'blk', axis=0, tiled=T...]
  transfers between devices with their start and end apart: 4 -> 0, of which waited for: 4 -> 0; matrix products, arithmetic and copies ran while one was open for 3% -> 0% of each run, Pallas kernels for 0% -> 0%
where the time goes in v1:
time: 81 us; the launch traced here: 80 us
  Pallas kernels  74.4 us (92%)
  local copies, waits for them, and re-layouts  4.92 us (6%)
    pallas_call x1, Pallas kernels, shards(): pl.pallas_call(kernel, out_shape=(jax.ShapeDtypeStruct((384, 2048), BF16)...  74.4 us
    unnamed x7, local copies, waits for them, and re-layouts  4.92 us

profile of v1, /device:TPU:2, one launch (start us, length us, event | category | flops | bytes accessed | tf_op | source)
XLA Modules:
  0.0 80.0 jit_solution(7534826000570596305)
XLA Ops:
  0.6 74.4 %kv_back.1 = (bf16[384,2048]{1,0:T(8,128)(2,1)}, bf16[384,1024]{1,0:T(8,128)(2,1)}, f32[512,256]{1,0:T(8,128)}) custom-call(bf16[384,8192]{1,0:T(8,128)(2,1)} %li.1, bf16[384,1024]{1,0:T(8,128)(2,1)} %q.1, bf16[384,128]{1,0:T(8,128)(2,1)} %k.1, bf16[384,128]{1,0:T(8,128)(2,1)} %v.1, bf16[512,256]{1,0:T(8,128)(2,1)} %w.1, bf16[384,1024]{1,0:T(8,128)(2,1)} %do.1, ...), custom_call_target="tpu_custom_call" | custom-call | flops 5000000000 | bytes 20000000 | tf_op jit(solution)/shard_map/kv_back/pallas_call | solution.py:422
  75.0 0.0 copy-start
  75.1 2.8 %copy.13 = bf16[384,2048]{1,0:T(8,128)(2,1)} copy(bf16[384,2048]{1,0:T(8,128)(2,1)} %get-tuple-element.6) | data formatting | bytes 3145728
  77.9 0.0 copy-done
  77.9 0.0 copy-start.1
  77.9 0.9 %copy.14 = bf16[384,1024]{1,0:T(8,128)(2,1)} copy(bf16[384,1024]{1,0:T(8,128)(2,1)S(1)} %copy-done) | data formatting | bytes 1572864
  78.7 0.4 copy-done.1
  79.2 0.8 copy.15
Async XLA Ops:
  75.0 2.8 %copy-start = (bf16[384,1024]{1,0:T(8,128)(2,1)S(1)}, bf16[384,1024]{1,0:T(8,128)(2,1)}, u32[]{:S(2)}) copy-start(bf16[384,1024]{1,0:T(8,128)(2,1)} %get-tuple-element.7) | copy-start | bytes 2359300
  77.9 1.3 %copy-start.1 = (f32[512,256]{1,0:T(8,128)S(1)}, f32[512,256]{1,0:T(8,128)}, u32[]{:S(2)}) copy-start(f32[512,256]{1,0:T(8,128)} %get-tuple-element.8) | copy-start | bytes 1572868

commit v2 on v1

v2 whole, which is shorter than its diff:
```python
import functools

import jax
import jax.numpy as jnp
from jax import lax
from jax.experimental import pallas as pl
from jax.experimental.pallas import tpu as pltpu
from jax.sharding import PartitionSpec as P

HD = 128
BY_USE = (4, 3, 5, 2, 6, 1, 7, 0)
MESH = pl.DeviceIdType.MESH
F32 = jnp.float32
BF16 = jnp.bfloat16


def device(x, y, z, c):
    return {"blk": (y % 2) * 8 + z, "tp": (y // 2) * 2 + c, "dp": x}


def dot(a, b, dims):
    return lax.dot_general(a, b, (dims, ((), ())), preferred_element_type=F32)


def kernel(
    li, q_in, k_in, v_in, w, do_in, dl,
    ig, qg, wg,
    q, k, v, do, xb, wz, wfull, kv_all, kv_oth, kvt, sbuf, rbuf, facc, xs, xr, fin, wgt,
    igo, igi, bias, kacc, vacc,
    in_sem, xo_sem, xs_s, xs_r, xsib_s, xsib_r,
    w0_s, w0_r, wz_s, wz_r, wx_s, wx_r, wsib_s, wsib_r, wloc,
    k1_s, k1_r, k2_s, k2_r, ks_s, ks_r, ko_s, ko_r,
    rs_s, rs_r, xr_s, xr_r, fin_s, fin_r, ig_s, ig_r,
):
    blk, tp, x = lax.axis_index("blk"), lax.axis_index("tp"), lax.axis_index("dp")
    yl, z, yh, c = blk // 8, blk % 8, tp // 2, tp % 2
    y = yh * 2 + yl
    p = x % 2

    def remote(src, dst, ssem, rsem, dev):
        return pltpu.make_async_remote_copy(
            src_ref=src, dst_ref=dst, send_sem=ssem, recv_sem=rsem,
            device_id=dev, device_id_type=MESH,
        )

    def at(dx=0, dy=0, dz=0, core=None):
        return device((x + dx) % 4, (y + dy) % 4, (z + dz) % 8, c if core is None else core)

    sibling = at(core=1 - c)

    partners = [at(dz=1), at(dz=7), sibling, at(dy=1), at(dy=2), at(dy=3), at(dx=2)]
    for dx in (1, 3):
        for core in (0, 1):
            partners.append(at(dx=dx, core=core))
    for dx in (1, 2, 3):
        for dy in (1, 3):
            partners.append(at(dx=dx, dy=dy))
    barrier = pltpu.get_barrier_semaphore()
    for d in partners:
        pl.semaphore_signal(barrier, inc=1, device_id=d, device_id_type=MESH)

    def x_own(zp):
        cols = pl.ds(pl.multiple_of(((1 - yl) * 8 + zp) * 512 + yh * 256, 256), 256)
        return pltpu.make_async_copy(li.at[:, cols], xb.at[zp, pl.ds(0, 384)], xo_sem.at[zp])

    loads = [
        pltpu.make_async_copy(a, b, in_sem.at[i])
        for i, (a, b) in enumerate(((q_in, q), (k_in, k), (v_in, v), (do_in, do)))
    ]
    for load in loads:
        load.start()

    pl.semaphore_wait(barrier, len(partners))

    rows_p = pl.ds(pl.multiple_of(p * 128, 128), 128)
    rows_o = pl.ds(pl.multiple_of((1 - p) * 128, 128), 128)

    def w0_rows(i):
        return w.at[pl.ds(pl.multiple_of(256 * i + p * 128, 128), 128)]

    def w0_remote(i):
        return remote(
            w0_rows(i), wz.at[z, yh], w0_s.at[i], w0_r.at[yh],
            device(x, 2 * yl + i, z, c),
        )

    def w0_local(i):
        return pltpu.make_async_copy(w0_rows(i), wz.at[z, yh], w0_r.at[yh])

    for i in range(2):
        @pl.when(2 * yl + i != y)
        def _():
            w0_remote(i).start()

        @pl.when(2 * yl + i == y)
        def _():
            w0_local(i).start()

    def x_send(side, zp):
        ydst = (y + 1) % 4 if side == 0 else (y + 3) % 4
        cols = pl.ds(pl.multiple_of((yl * 8 + zp) * 512 + (ydst // 2) * 256, 256), 256)
        return remote(
            li.at[pl.ds(192 * side, 192), cols],
            xb.at[zp, pl.ds(384 + 192 * side, 192)],
            xs_s.at[side, zp % 4], xs_r.at[side, zp % 4], device(x, ydst, z, c),
        )

    def x_relay(zp):
        ref = xb.at[zp, pl.ds(384, 384)]
        return remote(ref, ref, xsib_s.at[zp % 4], xsib_r.at[zp % 4], sibling)

    def block(dz):
        return (z + dz) % 8

    for dz in BY_USE:
        zp = block(dz)

        @pl.when(zp // 4 == c)
        def _():
            for side in range(2):
                x_send(side, zp).start()

    for dz in BY_USE:
        x_own(block(dz)).start()

    def x_pass(dz):
        zp = block(dz)

        @pl.when(zp // 4 == c)
        def _():
            for side in range(2):
                x_send(side, zp).wait_recv()
            x_relay(zp).start()

    def x_ready(dz):
        zp = block(dz)
        x_own(zp).wait()

        @pl.when(zp // 4 != c)
        def _():
            x_relay(zp).wait_recv()

    def spread_x(zp, side):
        j, cz = zp % 4, zp // 4
        return remote(
            wz.at[zp, side], wfull.at[j, c, side, rows_p],
            wx_s.at[zp, side], wx_r.at[j, c, side],
            at(dx=1 if side == 0 else 3, core=cz),
        )

    def spread_sibling(zp):
        j = zp % 4
        return remote(
            wz.at[zp], wfull.at[j, c, :, rows_p], wsib_s.at[zp], wsib_r.at[j], sibling
        )

    def spread_local(zp):
        j = zp % 4
        return pltpu.make_async_copy(wz.at[zp], wfull.at[j, c, :, rows_p], wloc.at[j])

    def spread(zp):
        for side in range(2):
            spread_x(zp, side).start()

        @pl.when(zp // 4 == c)
        def _():
            spread_local(zp).start()

        @pl.when(zp // 4 != c)
        def _():
            spread_sibling(zp).start()

    def wz_copy(direction, s):
        zp = (z - s + 8) % 8 if direction == 0 else (z + s) % 8
        ref = wz.at[zp, direction] if s == 3 else wz.at[zp]
        return remote(
            ref, ref, wz_s.at[direction, s], wz_r.at[direction, s],
            at(dz=1 if direction == 0 else 7),
        )

    def wz_wait(direction, s):
        zp = (z - s + 7) % 8 if direction == 0 else (z + s + 1) % 8
        ref = wz.at[zp, direction] if s == 3 else wz.at[zp]
        remote(ref, ref, wz_s.at[direction, s], wz_r.at[direction, s], sibling).wait_recv()
        return zp

    def w_begin():
        for h in range(2):
            remote(w0_rows(0), wz.at[z, h], w0_s.at[h], w0_r.at[h], sibling).wait_recv()
        for direction in range(2):
            wz_copy(direction, 0).start()
        spread(z)

    def w_step(s):
        arrived = [wz_wait(direction, s) for direction in range(2)]
        if s < 3:
            for direction in range(2):
                wz_copy(direction, s + 1).start()
            for zp in arrived:
                spread(zp)
        else:
            spread(arrived[0])

    lens = [dl[0, i] for i in range(3)]
    ends = [lens[0], lens[0] + lens[1], lens[0] + lens[1] + lens[2]]

    def documents(shape, dim):
        pos = lax.broadcasted_iota(jnp.int32, shape, dim)
        return pos, sum((pos >= e).astype(jnp.int32) for e in ends)

    kpos, kdoc = documents((384, 1), 0)
    qpos, qdoc = documents((1, 384), 1)
    bias[...] = jnp.where((kdoc == qdoc) & (kpos <= qpos), 0.0, -1e30).astype(F32)
    kacc[...] = jnp.zeros_like(kacc)
    vacc[...] = jnp.zeros_like(vacc)
    scale = 1.0 / HD**0.5

    def head(h, carry):
        lanes = pl.ds(pl.multiple_of(h * HD, HD), HD)
        for b in range(3):
            n = 128 * (b + 1)
            rows = pl.ds(128 * b, 128)
            qb, gb = q[rows, lanes], do[rows, lanes]
            s = dot(k[:n], qb, ((1,), (1,))) + bias[:n, 128 * b:n]
            e = jnp.exp((s - jnp.max(s, axis=0, keepdims=True)) * scale)
            probs = e * (1.0 / jnp.sum(e, axis=0, keepdims=True))
            pg = dot(v[:n], gb, ((1,), (1,)))
            inner = jnp.sum(probs * pg, axis=0, keepdims=True)
            ds = (probs * (pg - inner) * scale).astype(BF16)
            qg[rows, lanes] = dot(ds, k[:n], ((0,), (0,))).astype(BF16)
            kacc[:n] += dot(ds, qb, ((1,), (0,)))
            vacc[:n] += dot(probs.astype(BF16), gb, ((1,), (0,)))
        return carry

    for load in loads:
        load.wait()
    lax.fori_loop(0, 2, head, 0)
    w_begin()
    lax.fori_loop(2, 5, head, 0)
    for dz in BY_USE[:3]:
        x_pass(dz)
    lax.fori_loop(5, 8, head, 0)

    kv_all[c, yh, :, :HD] = kacc[...].astype(BF16)
    kv_all[c, yh, :, HD:] = vacc[...].astype(BF16)

    def kv1(side):
        return remote(
            kv_all.at[c, yh], kv_oth.at[c, yh], k1_s.at[side], k1_r.at[yh],
            at(dy=1 if side == 0 else 3),
        )

    for side in range(2):
        kv1(side).start()

    def kv_sibling(i):
        ref = kv_all.at[c, yh] if i == 0 else kv_all.at[c, 1 - yh]
        return remote(ref, ref, ks_s.at[i], ks_r.at[i], sibling)

    kv_sibling(0).start()

    def kv2(side):
        hsrc = ((y + 3) % 4) // 2 if side == 0 else ((y + 1) % 4) // 2
        rows = pl.ds(192 * side, 192)
        return remote(
            kv_oth.at[c, hsrc, rows], kv_all.at[c, hsrc, rows], k2_s.at[side], k2_r.at[side],
            at(dy=1 if side == 0 else 3),
        )

    def transpose_kv(h):
        kvt[h, :, :384] = kv_all[c, h].astype(F32).T.astype(BF16)
        kvt[h, :, 384:] = kv_oth[c, h].astype(F32).T.astype(BF16)

    def partial(f, zp, first=0, count=128):
        h = yh if f < 2 else 1 - yh
        first += 128 * (f % 2)
        return dot(kvt[h, first:first + count, :], xb[zp], ((1,), (0,)))

    def rs_copy(f, direction, s):
        half = pl.ds(0, 64) if s == 0 else pl.ds(0, 128)
        return remote(
            sbuf.at[f, direction, s, half], rbuf.at[f, direction, s, half],
            rs_s.at[f, direction, s], rs_r.at[f, direction, s],
            at(dz=1 if direction == 0 else 7),
        )

    def rs_step(f, s):
        terms = []
        for direction in range(2):
            zd = (z + 4 - s) % 8 if direction == 0 else (z + 4 + s) % 8
            if s == 0:
                terms.append(partial(f, zd, 64 * direction, 64))
            else:
                terms.append(partial(f, zd))
        for direction in range(2):
            term = terms[direction]
            if s == 0:
                sbuf[f, direction, 0, :64] = term.astype(BF16)
            else:
                rs_copy(f, direction, s - 1).wait_recv()
                if s == 1:
                    mine = slice(64 * direction, 64 * direction + 64)
                    rest = slice(64 - 64 * direction, 128 - 64 * direction)
                    sbuf[f, direction, 1, rest] = term[rest].astype(BF16)
                    sbuf[f, direction, 1, mine] = (
                        term[mine] + rbuf[f, direction, 0, :64].astype(F32)
                    ).astype(BF16)
                else:
                    sbuf[f, direction, s] = (
                        term + rbuf[f, direction, s - 1].astype(F32)
                    ).astype(BF16)
            rs_copy(f, direction, s).start()

    def rs_last(f):
        total = partial(f, z)
        for direction in range(2):
            rs_copy(f, direction, 3).wait_recv()
            total = total + rbuf[f, direction, 3].astype(F32)
        half = slice(128 * (f % 2), 128 * (f % 2) + 128)
        facc[f // 2, half] = total
        xs[f // 2, half] = total.astype(BF16)

    def x_copy(i, n):
        quarter = pl.ds(pl.multiple_of(((x + n) % 4) * 64, 64), 64)
        return remote(
            xs.at[i, quarter], xr.at[i, n - 1], xr_s.at[i, n - 1], xr_r.at[i, n - 1], at(dx=n)
        )

    def x_first(i):
        for n in (2, 1, 3):
            x_copy(i, n).start()

    def fin_copy(i, n):
        h = yh if i == 0 else 1 - yh
        cols = pl.ds(pl.multiple_of(x * 64, 64), 64)
        return remote(
            fin.at[i], wgt.at[yh, cols], fin_s.at[i, n], fin_r.at[yh, x],
            device((x + n) % 4, 2 * h + 1 - yl, z, c),
        )

    def x_last(i):
        total = facc[i, pl.ds(pl.multiple_of(x * 64, 64), 64)]
        for n in range(1, 4):
            x_copy(i, n).wait_recv()
            total = total + xr[i, n - 1].astype(F32)
        fin[i] = total.astype(BF16)
        for n in (2, 1, 3, 0):
            fin_copy(i, n).start()

    def w_ready(j):
        pltpu.make_async_copy(wz.at[0], wfull.at[j, c, :, rows_p], wloc.at[j]).wait()
        remote(
            wz.at[0], wfull.at[j, 1 - c, :, rows_p], wsib_s.at[0], wsib_r.at[j], sibling
        ).wait_recv()
        for cc in range(2):
            for side in range(2):
                remote(
                    wz.at[0, side], wfull.at[j, cc, side, rows_o],
                    wx_s.at[0, side], wx_r.at[j, cc, side], sibling,
                ).wait_recv()

    def ig_copy(j):
        return remote(
            igo.at[j], igi.at[j], ig_s.at[j], ig_r.at[j], device(x, 2 * yh + 1 - yl, z, c)
        )

    def ig_step(j):
        w_ready(j)

        def rows_of(kv):
            total = None
            for cc in range(2):
                for h in range(2):
                    term = dot(kv[cc, h], wfull[j, cc, h], ((1,), (1,)))
                    total = term if total is None else total + term
            return total.astype(BF16)

        igo[j] = rows_of(kv_oth)
        ig_copy(j).start()
        ig[:, pl.ds(pl.multiple_of(512 * j + 256 * yl, 256), 256)] = rows_of(kv_all)

    def ig_last(j):
        ig_copy(j).wait_recv()
        ig[:, pl.ds(pl.multiple_of(512 * j + 256 * (1 - yl), 256), 256)] = igi[j]

    def kv_own_sibling(i):
        ref = kv_all.at[1 - c, yh] if i == 0 else kv_all.at[1 - c, 1 - yh]
        remote(ref, ref, ks_s.at[i], ks_r.at[i], sibling).wait_recv()

    def kv_other(core):
        return remote(kv_oth.at[core], kv_oth.at[core], ko_s, ko_r, sibling)

    for dz in BY_USE[3:]:
        x_pass(dz)
    w_step(0)
    w_step(1)
    for h in range(2):
        remote(
            kv_all.at[c, yh], kv_oth.at[c, h], k1_s.at[h], k1_r.at[h], sibling
        ).wait_recv()
    for side in range(2):
        kv2(side).start()
    kv_other(c).start()
    transpose_kv(yh)
    x_ready(4)
    rs_step(0, 0)
    rs_step(1, 0)
    w_step(2)
    x_ready(3)
    x_ready(5)
    rs_step(0, 1)
    rs_step(1, 1)
    for side in range(2):
        rows = pl.ds(192 * side, 192)
        remote(
            kv_oth.at[c, 0, rows], kv_all.at[c, 1 - yh, rows], k2_s.at[side], k2_r.at[side],
            sibling,
        ).wait_recv()
    kv_sibling(1).start()
    transpose_kv(1 - yh)
    rs_step(2, 0)
    rs_step(3, 0)
    x_ready(2)
    x_ready(6)
    rs_step(0, 2)
    rs_step(1, 2)
    w_step(3)
    rs_step(2, 1)
    rs_step(3, 1)
    for i in range(2):
        kv_own_sibling(i)
    kv_other(1 - c).wait_recv()
    ig_step(0)
    x_ready(1)
    x_ready(7)
    rs_step(0, 3)
    rs_step(1, 3)
    ig_step(1)
    rs_step(2, 2)
    rs_step(3, 2)
    ig_step(2)
    x_ready(0)
    rs_last(0)
    rs_last(1)
    x_first(0)
    ig_step(3)
    rs_step(2, 3)
    rs_step(3, 3)
    x_last(0)
    rs_last(2)
    rs_last(3)
    x_first(1)
    for j in range(3):
        ig_last(j)
    x_last(1)
    ig_last(3)

    for hs in range(2):
        for xx in range(4):
            remote(
                fin.at[0], wgt.at[hs, pl.ds(64 * xx, 64)], fin_s.at[0, 0], fin_r.at[hs, xx], sibling
            ).wait_recv()
        wg[256 * hs:256 * hs + 256, :] = wgt[hs].astype(F32).T

    for i in range(2):
        @pl.when(2 * yl + i != y)
        def _():
            w0_remote(i).wait_send()
    for side in range(2):
        kv1(side).wait_send()
        kv2(side).wait_send()
        kv_sibling(side).wait_send()
        for s in range(4):
            wz_copy(side, s).wait_send()
            for f in range(4):
                rs_copy(f, side, s).wait_send()
    kv_other(c).wait_send()
    for j in range(4):
        zp = 4 * c + j
        for side in range(2):
            x_send(side, zp).wait_send()
        x_relay(zp).wait_send()
        ig_copy(j).wait_send()
    for zp in range(8):
        for side in range(2):
            spread_x(zp, side).wait_send()

        @pl.when(zp // 4 != c)
        def _():
            spread_sibling(zp).wait_send()
    for i in range(2):
        for n in range(1, 4):
            x_copy(i, n).wait_send()
        for n in range(4):
            fin_copy(i, n).wait_send()


def shards(layer_input, queries, keys, values, kv_weight, out_grad, doc_lengths):
    vmem = pl.BlockSpec(memory_space=pltpu.VMEM)
    hbm = pl.BlockSpec(memory_space=pl.ANY)
    smem = pl.BlockSpec(memory_space=pltpu.SMEM)
    dma = pltpu.SemaphoreType.DMA
    return pl.pallas_call(
        kernel,
        out_shape=(
            jax.ShapeDtypeStruct((384, 2048), BF16),
            jax.ShapeDtypeStruct((384, 1024), BF16),
            jax.ShapeDtypeStruct((512, 256), F32),
        ),
        in_specs=[hbm, hbm, hbm, hbm, hbm, hbm, smem],
        out_specs=(vmem, vmem, vmem),
        scratch_shapes=[
            pltpu.VMEM((384, 1024), BF16),
            pltpu.VMEM((384, 128), BF16),
            pltpu.VMEM((384, 128), BF16),
            pltpu.VMEM((384, 1024), BF16),
            pltpu.VMEM((8, 768, 256), BF16),
            pltpu.VMEM((8, 2, 128, 256), BF16),
            pltpu.VMEM((4, 2, 2, 256, 256), BF16),
            pltpu.VMEM((2, 2, 384, 256), BF16),
            pltpu.VMEM((2, 2, 384, 256), BF16),
            pltpu.VMEM((2, 256, 768), BF16),
            pltpu.VMEM((4, 2, 4, 128, 256), BF16),
            pltpu.VMEM((4, 2, 4, 128, 256), BF16),
            pltpu.VMEM((2, 256, 256), F32),
            pltpu.VMEM((2, 256, 256), BF16),
            pltpu.VMEM((2, 3, 64, 256), BF16),
            pltpu.VMEM((2, 64, 256), BF16),
            pltpu.VMEM((2, 256, 256), BF16),
            pltpu.VMEM((4, 384, 256), BF16),
            pltpu.VMEM((4, 384, 256), BF16),
            pltpu.VMEM((384, 384), F32),
            pltpu.VMEM((384, 128), F32),
            pltpu.VMEM((384, 128), F32),
            dma((4,)), dma((8,)), dma((2, 4)), dma((2, 4)), dma((4,)), dma((4,)),
            dma((2,)), dma((2,)), dma((2, 4)), dma((2, 4)),
            dma((8, 2)), dma((4, 2, 2)), dma((8,)), dma((4,)), dma((4,)),
            dma((2,)), dma((2,)), dma((2,)), dma((2,)), dma((2,)), dma((2,)), dma, dma,
            dma((4, 2, 4)), dma((4, 2, 4)), dma((2, 3)), dma((2, 3)),
            dma((2, 4)), dma((2, 4)), dma((4,)), dma((4,)),
        ],
        compiler_params=pltpu.CompilerParams(
            collective_id=0, has_side_effects=True, vmem_limit_bytes=56 << 20
        ),
        cost_estimate=pl.CostEstimate(
            flops=5 * 10**9, bytes_accessed=2 * 10**7, transcendentals=10**6
        ),
        name="kv_back",
    )(layer_input, queries, keys, values, kv_weight, out_grad, doc_lengths)


def solution(mesh):
    placed = (
        P(("blk", "dp"), None),
        P(("blk", "dp"), "tp"),
        P(("blk", "dp"), "tp"),
        P(("blk", "dp"), "tp"),
        P("blk", "tp"),
        P(("blk", "dp"), "tp"),
        P(("blk", "dp"), None),
    )
    return jax.shard_map(
        shards,
        mesh=mesh,
        in_specs=placed,
        out_specs=(P(("blk", "dp"), "tp"), P(("blk", "dp"), "tp"), P("blk", "tp")),
        check_vma=False,
    )
```

time: 81 us -> 77.2 us (0.953)
  Pallas kernels: 74.4 us -> 70.7 us
    pallas_call x1, Pallas kernels: 74.4 us -> 70.7 us  [shards(): pl.pallas_call(kernel, out_shape=(jax.ShapeDtypeStruct((384, 2048), BF16)...]
where the time goes in v2:
time: 77.2 us; the launch traced here: 76.2 us
  Pallas kernels  70.7 us (92%)
  local copies, waits for them, and re-layouts  4.92 us (6%)
    pallas_call x1, Pallas kernels, shards(): pl.pallas_call(kernel, out_shape=(jax.ShapeDtypeStruct((384, 2048), BF16)...  70.7 us
    unnamed x7, local copies, waits for them, and re-layouts  4.92 us

profile of v2, /device:TPU:2, one launch (start us, length us, event | category | flops | bytes accessed | tf_op | source)
XLA Modules:
  0.0 76.2 jit_solution(1017924893268353616)
XLA Ops:
  0.6 70.7 %kv_back.1 = (bf16[384,2048]{1,0:T(8,128)(2,1)}, bf16[384,1024]{1,0:T(8,128)(2,1)}, f32[512,256]{1,0:T(8,128)}) custom-call(bf16[384,8192]{1,0:T(8,128)(2,1)} %li.1, bf16[384,1024]{1,0:T(8,128)(2,1)} %q_in.1, bf16[384,128]{1,0:T(8,128)(2,1)} %k_in.1, bf16[384,128]{1,0:T(8,128)(2,1)} %v_in.1, bf16[512,256]{1,0:T(8,128)(2,1)} %w.1, bf16[384,1024]{1,0:T(8,128)(2,1)} %do_in.1, ...), custom_call_target="tpu_custom_call" | custom-call | flops 5000000000 | bytes 20000000 | tf_op jit(solution)/shard_map/kv_back/pallas_call | solution.py:503
  71.3 0.0 copy-start
  71.3 2.8 %copy.13 = bf16[384,2048]{1,0:T(8,128)(2,1)} copy(bf16[384,2048]{1,0:T(8,128)(2,1)} %get-tuple-element.6) | data formatting | bytes 3145728
  74.1 0.0 copy-done
  74.1 0.0 copy-start.1
  74.1 0.9 %copy.14 = bf16[384,1024]{1,0:T(8,128)(2,1)} copy(bf16[384,1024]{1,0:T(8,128)(2,1)S(1)} %copy-done) | data formatting | bytes 1572864
  75.0 0.4 copy-done.1
  75.5 0.8 %copy.15 = f32[512,256]{1,0:T(8,128)} copy(f32[512,256]{1,0:T(8,128)S(1)} %copy-done.1) | data formatting | bytes 1048576
Async XLA Ops:
  71.3 2.8 %copy-start = (bf16[384,1024]{1,0:T(8,128)(2,1)S(1)}, bf16[384,1024]{1,0:T(8,128)(2,1)}, u32[]{:S(2)}) copy-start(bf16[384,1024]{1,0:T(8,128)(2,1)} %get-tuple-element.7) | copy-start | bytes 2359300
  74.1 1.3 %copy-start.1 = (f32[512,256]{1,0:T(8,128)S(1)}, f32[512,256]{1,0:T(8,128)}, u32[]{:S(2)}) copy-start(f32[512,256]{1,0:T(8,128)} %get-tuple-element.8) | copy-start | bytes 1572868

commit v3 on v2

--- a/solution.py
+++ b/solution.py
@@ -24,12 +24,12 @@
 
 def kernel(
     li, q_in, k_in, v_in, w, do_in, dl,
-    ig, qg, wg,
-    q, k, v, do, xb, wz, wfull, kv_all, kv_oth, kvt, sbuf, rbuf, facc, xs, xr, fin, wgt,
-    igo, igi, bias, kacc, vacc,
-    in_sem, xo_sem, xs_s, xs_r, xsib_s, xsib_r,
+    ig_out, qg_out, wg_out,
+    q, k, v, do, probs, qg, xb, wz, wfull, kv_all, kv_oth, kvt, sbuf, rbuf, facc, xs, xr, fin, wgt,
+    iga, igo, igi, bias, kacc, vacc,
+    in_sem, out_sem, xo_sem, xs_s, xs_r, xsib_s, xsib_r,
     w0_s, w0_r, wz_s, wz_r, wx_s, wx_r, wsib_s, wsib_r, wloc,
-    k1_s, k1_r, k2_s, k2_r, ks_s, ks_r, ko_s, ko_r,
+    k1_s, k1_r, k2_s, k2_r, ks_s, ks_r,
     rs_s, rs_r, xr_s, xr_r, fin_s, fin_r, ig_s, ig_r,
 ):
     blk, tp, x = lax.axis_index("blk"), lax.axis_index("tp"), lax.axis_index("dp")
@@ -215,65 +215,81 @@
     vacc[...] = jnp.zeros_like(vacc)
     scale = 1.0 / HD**0.5
 
-    def head(h, carry):
+    def value_head(h, carry):
         lanes = pl.ds(pl.multiple_of(h * HD, HD), HD)
         for b in range(3):
             n = 128 * (b + 1)
             rows = pl.ds(128 * b, 128)
-            qb, gb = q[rows, lanes], do[rows, lanes]
-            s = dot(k[:n], qb, ((1,), (1,))) + bias[:n, 128 * b:n]
+            s = dot(k[:n], q[rows, lanes], ((1,), (1,))) + bias[:n, 128 * b:n]
             e = jnp.exp((s - jnp.max(s, axis=0, keepdims=True)) * scale)
-            probs = e * (1.0 / jnp.sum(e, axis=0, keepdims=True))
-            pg = dot(v[:n], gb, ((1,), (1,)))
-            inner = jnp.sum(probs * pg, axis=0, keepdims=True)
-            ds = (probs * (pg - inner) * scale).astype(BF16)
+            soft = e * (1.0 / jnp.sum(e, axis=0, keepdims=True))
+            probs[h, :n, 128 * b:n] = soft
+            vacc[:n] += dot(soft.astype(BF16), do[rows, lanes], ((1,), (0,)))
+        return carry
+
+    def key_head(h, carry):
+        lanes = pl.ds(pl.multiple_of(h * HD, HD), HD)
+        for b in range(3):
+            n = 128 * (b + 1)
+            rows = pl.ds(128 * b, 128)
+            soft = probs[h, :n, 128 * b:n]
+            pg = dot(v[:n], do[rows, lanes], ((1,), (1,)))
+            inner = jnp.sum(soft * pg, axis=0, keepdims=True)
+            ds = (soft * (pg - inner) * scale).astype(BF16)
             qg[rows, lanes] = dot(ds, k[:n], ((0,), (0,))).astype(BF16)
-            kacc[:n] += dot(ds, qb, ((1,), (0,)))
-            vacc[:n] += dot(probs.astype(BF16), gb, ((1,), (0,)))
+            kacc[:n] += dot(ds, q[rows, lanes], ((1,), (0,)))
         return carry
 
-    for load in loads:
-        load.wait()
-    lax.fori_loop(0, 2, head, 0)
-    w_begin()
-    lax.fori_loop(2, 5, head, 0)
-    for dz in BY_USE[:3]:
-        x_pass(dz)
-    lax.fori_loop(5, 8, head, 0)
-
-    kv_all[c, yh, :, :HD] = kacc[...].astype(BF16)
-    kv_all[c, yh, :, HD:] = vacc[...].astype(BF16)
-
-    def kv1(side):
-        return remote(
-            kv_all.at[c, yh], kv_oth.at[c, yh], k1_s.at[side], k1_r.at[yh],
-            at(dy=1 if side == 0 else 3),
-        )
-
-    for side in range(2):
-        kv1(side).start()
-
-    def kv_sibling(i):
-        ref = kv_all.at[c, yh] if i == 0 else kv_all.at[c, 1 - yh]
-        return remote(ref, ref, ks_s.at[i], ks_r.at[i], sibling)
-
-    kv_sibling(0).start()
-
-    def kv2(side):
+    def part(i):
+        return pl.ds(128 * (1 - i), 128)
+
+    def kv1(i, side):
+        return remote(
+            kv_all.at[c, yh, :, part(i)], kv_oth.at[c, yh, :, part(i)],
+            k1_s.at[i, side], k1_r.at[i, yh], at(dy=1 if side == 0 else 3),
+        )
+
+    def kv1_start(i, acc):
+        kv_all[c, yh, :, part(i)] = acc[...].astype(BF16)
+        for side in range(2):
+            kv1(i, side).start()
+
+    def kv2(i, side):
         hsrc = ((y + 3) % 4) // 2 if side == 0 else ((y + 1) % 4) // 2
         rows = pl.ds(192 * side, 192)
         return remote(
-            kv_oth.at[c, hsrc, rows], kv_all.at[c, hsrc, rows], k2_s.at[side], k2_r.at[side],
-            at(dy=1 if side == 0 else 3),
-        )
-
-    def transpose_kv(h):
-        kvt[h, :, :384] = kv_all[c, h].astype(F32).T.astype(BF16)
-        kvt[h, :, 384:] = kv_oth[c, h].astype(F32).T.astype(BF16)
+            kv_oth.at[c, hsrc, rows, part(i)], kv_all.at[c, hsrc, rows, part(i)],
+            k2_s.at[i, side], k2_r.at[i, side], at(dy=1 if side == 0 else 3),
+        )
+
+    def transpose_kv(i, h):
+        kvt[h, part(i), :384] = kv_all[c, h, :, part(i)].astype(F32).T.astype(BF16)
+        kvt[h, part(i), 384:] = kv_oth[c, h, :, part(i)].astype(F32).T.astype(BF16)
+
+    def kv1_ready(i):
+        for h in range(2):
+            remote(
+                kv_oth.at[c, h, :, part(i)], kv_oth.at[c, h, :, part(i)],
+                k1_s.at[i, h], k1_r.at[i, h], sibling,
+            ).wait_recv()
+        for side in range(2):
+            kv2(i, side).start()
+        transpose_kv(i, yh)
+
+    def kv2_ready(i):
+        for side in range(2):
+            rows = pl.ds(192 * side, 192)
+            ref = kv_all.at[c, 1 - yh, rows, part(i)]
+            remote(ref, ref, k2_s.at[i, side], k2_r.at[i, side], sibling).wait_recv()
+        transpose_kv(i, 1 - yh)
+
+    def kv_sibling(i, core):
+        ref = (kv_all.at[core, yh], kv_all.at[core, 1 - yh], kv_oth.at[core])[i]
+        return remote(ref, ref, ks_s.at[i], ks_r.at[i], sibling)
 
     def partial(f, zp, first=0, count=128):
-        h = yh if f < 2 else 1 - yh
-        first += 128 * (f % 2)
+        h = yh if f % 2 == 0 else 1 - yh
+        first += 128 * (1 - f // 2)
         return dot(kvt[h, first:first + count, :], xb[zp], ((1,), (0,)))
 
     def rs_copy(f, direction, s):
@@ -316,36 +332,37 @@
         for direction in range(2):
             rs_copy(f, direction, 3).wait_recv()
             total = total + rbuf[f, direction, 3].astype(F32)
-        half = slice(128 * (f % 2), 128 * (f % 2) + 128)
-        facc[f // 2, half] = total
-        xs[f // 2, half] = total.astype(BF16)
+        facc[f // 2, f % 2] = total
+        xs[f // 2, f % 2] = total.astype(BF16)
 
     def x_copy(i, n):
-        quarter = pl.ds(pl.multiple_of(((x + n) % 4) * 64, 64), 64)
-        return remote(
-            xs.at[i, quarter], xr.at[i, n - 1], xr_s.at[i, n - 1], xr_r.at[i, n - 1], at(dx=n)
+        quarter = pl.ds(pl.multiple_of(((x + n) % 4) * 32, 32), 32)
+        return remote(
+            xs.at[i, :, quarter], xr.at[i, n - 1], xr_s.at[i, n - 1], xr_r.at[i, n - 1],
+            at(dx=n),
         )
 
     def x_first(i):
         for n in (2, 1, 3):
             x_copy(i, n).start()
 
-    def fin_copy(i, n):
-        h = yh if i == 0 else 1 - yh
-        cols = pl.ds(pl.multiple_of(x * 64, 64), 64)
-        return remote(
-            fin.at[i], wgt.at[yh, cols], fin_s.at[i, n], fin_r.at[yh, x],
+    def fin_copy(i, slot, n):
+        h = yh if slot == 0 else 1 - yh
+        cols = pl.ds(pl.multiple_of(128 * (1 - i) + x * 32, 32), 32)
+        return remote(
+            fin.at[i, slot], wgt.at[yh, cols], fin_s.at[i, slot, n], fin_r.at[i, yh, x],
             device((x + n) % 4, 2 * h + 1 - yl, z, c),
         )
 
     def x_last(i):
-        total = facc[i, pl.ds(pl.multiple_of(x * 64, 64), 64)]
+        total = facc[i, :, pl.ds(pl.multiple_of(x * 32, 32), 32)]
         for n in range(1, 4):
             x_copy(i, n).wait_recv()
             total = total + xr[i, n - 1].astype(F32)
         fin[i] = total.astype(BF16)
         for n in (2, 1, 3, 0):
-            fin_copy(i, n).start()
+            for slot in range(2):
+                fin_copy(i, slot, n).start()
 
     def w_ready(j):
         pltpu.make_async_copy(wz.at[0], wfull.at[j, c, :, rows_p], wloc.at[j]).wait()
@@ -377,77 +394,83 @@
 
         igo[j] = rows_of(kv_oth)
         ig_copy(j).start()
-        ig[:, pl.ds(pl.multiple_of(512 * j + 256 * yl, 256), 256)] = rows_of(kv_all)
+        iga[j] = rows_of(kv_all)
+        ig_store(j, 0).start()
+
+    def ig_store(j, other):
+        half = yl if other == 0 else 1 - yl
+        cols = pl.ds(pl.multiple_of(512 * j + 256 * half, 256), 256)
+        src = iga.at[j] if other == 0 else igi.at[j]
+        return pltpu.make_async_copy(src, ig_out.at[:, cols], out_sem.at[2 * j + other])
 
     def ig_last(j):
         ig_copy(j).wait_recv()
-        ig[:, pl.ds(pl.multiple_of(512 * j + 256 * (1 - yl), 256), 256)] = igi[j]
-
-    def kv_own_sibling(i):
-        ref = kv_all.at[1 - c, yh] if i == 0 else kv_all.at[1 - c, 1 - yh]
-        remote(ref, ref, ks_s.at[i], ks_r.at[i], sibling).wait_recv()
-
-    def kv_other(core):
-        return remote(kv_oth.at[core], kv_oth.at[core], ko_s, ko_r, sibling)
-
+        ig_store(j, 1).start()
+
+    qg_store = pltpu.make_async_copy(qg, qg_out, out_sem.at[8])
+    wg_store = pltpu.make_async_copy(wgt, wg_out, out_sem.at[9])
+
+    for load in loads:
+        load.wait()
+    lax.fori_loop(0, 2, value_head, 0)
+    w_begin()
+    lax.fori_loop(2, 8, value_head, 0)
+    kv1_start(0, vacc)
+    lax.fori_loop(0, 2, key_head, 0)
+    for dz in BY_USE[:3]:
+        x_pass(dz)
+    w_step(0)
+    lax.fori_loop(2, 5, key_head, 0)
+    kv1_ready(0)
+    x_ready(4)
+    rs_step(0, 0)
+    lax.fori_loop(5, 8, key_head, 0)
+    kv1_start(1, kacc)
+    qg_store.start()
+    kv_sibling(0, c).start()
     for dz in BY_USE[3:]:
         x_pass(dz)
-    w_step(0)
     w_step(1)
-    for h in range(2):
-        remote(
-            kv_all.at[c, yh], kv_oth.at[c, h], k1_s.at[h], k1_r.at[h], sibling
-        ).wait_recv()
-    for side in range(2):
-        kv2(side).start()
-    kv_other(c).start()
-    transpose_kv(yh)
-    x_ready(4)
-    rs_step(0, 0)
-    rs_step(1, 0)
-    w_step(2)
     x_ready(3)
     x_ready(5)
     rs_step(0, 1)
-    rs_step(1, 1)
-    for side in range(2):
-        rows = pl.ds(192 * side, 192)
-        remote(
-            kv_oth.at[c, 0, rows], kv_all.at[c, 1 - yh, rows], k2_s.at[side], k2_r.at[side],
-            sibling,
-        ).wait_recv()
-    kv_sibling(1).start()
-    transpose_kv(1 - yh)
+    kv2_ready(0)
+    rs_step(1, 0)
+    kv1_ready(1)
+    kv_sibling(2, c).start()
     rs_step(2, 0)
-    rs_step(3, 0)
     x_ready(2)
     x_ready(6)
+    w_step(2)
     rs_step(0, 2)
-    rs_step(1, 2)
-    w_step(3)
+    rs_step(1, 1)
+    kv2_ready(1)
+    kv_sibling(1, c).start()
+    rs_step(3, 0)
     rs_step(2, 1)
-    rs_step(3, 1)
-    for i in range(2):
-        kv_own_sibling(i)
-    kv_other(1 - c).wait_recv()
-    ig_step(0)
     x_ready(1)
     x_ready(7)
     rs_step(0, 3)
-    rs_step(1, 3)
-    ig_step(1)
+    w_step(3)
+    rs_step(1, 2)
+    rs_step(3, 1)
     rs_step(2, 2)
-    rs_step(3, 2)
-    ig_step(2)
     x_ready(0)
     rs_last(0)
+    for i in range(3):
+        kv_sibling(i, 1 - c).wait_recv()
+    ig_step(0)
+    rs_step(1, 3)
+    rs_step(3, 2)
+    ig_step(1)
+    rs_step(2, 3)
     rs_last(1)
     x_first(0)
+    ig_step(2)
+    rs_step(3, 3)
+    rs_last(2)
     ig_step(3)
-    rs_step(2, 3)
-    rs_step(3, 3)
     x_last(0)
-    rs_last(2)
     rs_last(3)
     x_first(1)
     for j in range(3):
@@ -455,32 +478,37 @@
     x_last(1)
     ig_last(3)
 
-    for hs in range(2):
-        for xx in range(4):
-            remote(
-                fin.at[0], wgt.at[hs, pl.ds(64 * xx, 64)], fin_s.at[0, 0], fin_r.at[hs, xx], sibling
-            ).wait_recv()
-        wg[256 * hs:256 * hs + 256, :] = wgt[hs].astype(F32).T
+    for i in range(2):
+        for hs in range(2):
+            for xx in range(4):
+                cols = pl.ds(128 * (1 - i) + 32 * xx, 32)
+                remote(
+                    fin.at[0, 0], wgt.at[hs, cols], fin_s.at[0, 0, 0], fin_r.at[i, hs, xx], sibling
+                ).wait_recv()
+    wg_store.start()
 
     for i in range(2):
         @pl.when(2 * yl + i != y)
         def _():
             w0_remote(i).wait_send()
     for side in range(2):
-        kv1(side).wait_send()
-        kv2(side).wait_send()
-        kv_sibling(side).wait_send()
+        for i in range(2):
+            kv1(i, side).wait_send()
+            kv2(i, side).wait_send()
         for s in range(4):
             wz_copy(side, s).wait_send()
             for f in range(4):
                 rs_copy(f, side, s).wait_send()
-    kv_other(c).wait_send()
+    for i in range(3):
+        kv_sibling(i, c).wait_send()
     for j in range(4):
         zp = 4 * c + j
         for side in range(2):
             x_send(side, zp).wait_send()
         x_relay(zp).wait_send()
         ig_copy(j).wait_send()
+        for other in range(2):
+            ig_store(j, other).wait()
     for zp in range(8):
         for side in range(2):
             spread_x(zp, side).wait_send()
@@ -491,28 +519,59 @@
     for i in range(2):
         for n in range(1, 4):
             x_copy(i, n).wait_send()
-        for n in range(4):
-            fin_copy(i, n).wait_send()
+        for slot in range(2):
+            for n in range(4):
+                fin_copy(i, slot, n).wait_send()
+    qg_store.wait()
+    wg_store.wait()
+
+
+def finish(ig_in, qg_in, wgt_in, ig, qg, wg, igv, qgv, wgt, wgf, load, store):
+    pieces = [
+        (ig_in.at[pl.ds(96 * i, 96)], igv.at[pl.ds(96 * i, 96)], ig.at[pl.ds(96 * i, 96)])
+        for i in range(4)
+    ] + [
+        (qg_in.at[pl.ds(192 * i, 192)], qgv.at[pl.ds(192 * i, 192)], qg.at[pl.ds(192 * i, 192)])
+        for i in range(2)
+    ]
+    first = pltpu.make_async_copy(wgt_in, wgt, load.at[6])
+    first.start()
+    loads = [pltpu.make_async_copy(a, b, load.at[i]) for i, (a, b, _) in enumerate(pieces)]
+    stores = [pltpu.make_async_copy(b, o, store.at[i]) for i, (_, b, o) in enumerate(pieces)]
+    for copy in loads:
+        copy.start()
+    first.wait()
+    for hs in range(2):
+        wgf[256 * hs:256 * hs + 256, :] = wgt[hs].astype(F32).T
+    last = pltpu.make_async_copy(wgf, wg, store.at[6])
+    last.start()
+    for a, b in zip(loads, stores):
+        a.wait()
+        b.start()
+    for copy in stores:
+        copy.wait()
+    last.wait()
 
 
 def shards(layer_input, queries, keys, values, kv_weight, out_grad, doc_lengths):
-    vmem = pl.BlockSpec(memory_space=pltpu.VMEM)
     hbm = pl.BlockSpec(memory_space=pl.ANY)
     smem = pl.BlockSpec(memory_space=pltpu.SMEM)
     dma = pltpu.SemaphoreType.DMA
-    return pl.pallas_call(
+    results = pl.pallas_call(
         kernel,
         out_shape=(
             jax.ShapeDtypeStruct((384, 2048), BF16),
             jax.ShapeDtypeStruct((384, 1024), BF16),
-            jax.ShapeDtypeStruct((512, 256), F32),
+            jax.ShapeDtypeStruct((2, 256, 256), BF16),
         ),
         in_specs=[hbm, hbm, hbm, hbm, hbm, hbm, smem],
-        out_specs=(vmem, vmem, vmem),
+        out_specs=(hbm, hbm, hbm),
         scratch_shapes=[
             pltpu.VMEM((384, 1024), BF16),
             pltpu.VMEM((384, 128), BF16),
             pltpu.VMEM((384, 128), BF16),
+            pltpu.VMEM((384, 1024), BF16),
+            pltpu.VMEM((8, 384, 384), F32),
             pltpu.VMEM((384, 1024), BF16),
             pltpu.VMEM((8, 768, 256), BF16),
             pltpu.VMEM((8, 2, 128, 256), BF16),
@@ -522,22 +581,23 @@
             pltpu.VMEM((2, 256, 768), BF16),
             pltpu.VMEM((4, 2, 4, 128, 256), BF16),
             pltpu.VMEM((4, 2, 4, 128, 256), BF16),
-            pltpu.VMEM((2, 256, 256), F32),
+            pltpu.VMEM((2, 2, 128, 256), F32),
+            pltpu.VMEM((2, 2, 128, 256), BF16),
+            pltpu.VMEM((2, 3, 2, 32, 256), BF16),
+            pltpu.VMEM((2, 2, 32, 256), BF16),
             pltpu.VMEM((2, 256, 256), BF16),
-            pltpu.VMEM((2, 3, 64, 256), BF16),
-            pltpu.VMEM((2, 64, 256), BF16),
-            pltpu.VMEM((2, 256, 256), BF16),
+            pltpu.VMEM((4, 384, 256), BF16),
             pltpu.VMEM((4, 384, 256), BF16),
             pltpu.VMEM((4, 384, 256), BF16),
             pltpu.VMEM((384, 384), F32),
             pltpu.VMEM((384, 128), F32),
             pltpu.VMEM((384, 128), F32),
-            dma((4,)), dma((8,)), dma((2, 4)), dma((2, 4)), dma((4,)), dma((4,)),
+            dma((4,)), dma((10,)), dma((8,)), dma((2, 4)), dma((2, 4)), dma((4,)), dma((4,)),
             dma((2,)), dma((2,)), dma((2, 4)), dma((2, 4)),
             dma((8, 2)), dma((4, 2, 2)), dma((8,)), dma((4,)), dma((4,)),
-            dma((2,)), dma((2,)), dma((2,)), dma((2,)), dma((2,)), dma((2,)), dma, dma,
+            dma((2, 2)), dma((2, 2)), dma((2, 2)), dma((2, 2)), dma((3,)), dma((3,)),
             dma((4, 2, 4)), dma((4, 2, 4)), dma((2, 3)), dma((2, 3)),
-            dma((2, 4)), dma((2, 4)), dma((4,)), dma((4,)),
+            dma((2, 2, 4)), dma((2, 2, 4)), dma((4,)), dma((4,)),
         ],
         compiler_params=pltpu.CompilerParams(
             collective_id=0, has_side_effects=True, vmem_limit_bytes=56 << 20
@@ -547,6 +607,22 @@
         ),
         name="kv_back",
     )(layer_input, queries, keys, values, kv_weight, out_grad, doc_lengths)
+    return pl.pallas_call(
+        finish,
+        out_shape=(
+            jax.ShapeDtypeStruct((384, 2048), BF16),
+            jax.ShapeDtypeStruct((384, 1024), BF16),
+            jax.ShapeDtypeStruct((512, 256), F32),
+        ),
+        in_specs=[hbm, hbm, hbm],
+        out_specs=(hbm, hbm, hbm),
+        scratch_shapes=[
+            pltpu.VMEM((384, 2048), BF16), pltpu.VMEM((384, 1024), BF16),
+            pltpu.VMEM((2, 256, 256), BF16), pltpu.VMEM((512, 256), F32), dma((7,)), dma((7,)),
+        ],
+        compiler_params=pltpu.CompilerParams(vmem_limit_bytes=60 << 20),
+        name="finish",
+    )(*results)
 
 
 def solution(mesh):

time: 77.2 us -> 71.3 us (0.924); the launches traced: 76.2 us -> 71.2 us
  local copies, waits for them, and re-layouts: 4.92 us -> 0 us
    unnamed x7 -> x0, local copies, waits for them, and re-layouts: 4.92 us -> none
    pallas_call x1, Pallas kernels: 70.7 us -> 67.8 us  [shards(): pl.pallas_call(kernel, out_shape=(jax.ShapeDtypeStruct((384, 2048), BF16)...]
    pallas_call x0 -> x1, Pallas kernels: none -> 2.78 us  [shards(): pl.pallas_call(finish, out_shape=(jax.ShapeDtypeStruct((384, 2048), BF16)...]
where the time goes in v3:
time: 71.3 us; the launch traced here: 71.2 us
  Pallas kernels  70.5 us (99%)
    pallas_call x1, Pallas kernels, shards(): pl.pallas_call(kernel, out_shape=(jax.ShapeDtypeStruct((384, 2048), BF16)...  67.8 us
    pallas_call x1, Pallas kernels, shards(): pl.pallas_call(finish, out_shape=(jax.ShapeDtypeStruct((384, 2048), BF16)...  2.78 us

profile of v3, /device:TPU:2, one launch (start us, length us, event | category | flops | bytes accessed | tf_op | source)
XLA Modules:
  0.0 71.2 jit_solution(13112314131998618746)
XLA Ops:
  0.6 67.8 %kv_back.1 = (bf16[384,2048]{1,0:T(8,128)(2,1)}, bf16[384,1024]{1,0:T(8,128)(2,1)}, bf16[2,256,256]{2,1,0:T(8,128)(2,1)}) custom-call(bf16[384,8192]{1,0:T(8,128)(2,1)} %li.1, bf16[384,1024]{1,0:T(8,128)(2,1)} %q_in.1, bf16[384,128]{1,0:T(8,128)(2,1)} %k_in.1, bf16[384,128]{1,0:T(8,128)(2,1)} %v_in.1, bf16[512,256]{1,0:T(8,128)(2,1)} %w.1, ...), custom_call_target="tpu_custom_call" | custom-call | flops 5000000000 | bytes 20000000 | tf_op jit(solution)/shard_map/kv_back/pallas_call | solution.py:560
  68.4 2.8 %finish.1 = (bf16[384,2048]{1,0:T(8,128)(2,1)}, bf16[384,1024]{1,0:T(8,128)(2,1)}, f32[512,256]{1,0:T(8,128)}) custom-call(bf16[384,2048]{1,0:T(8,128)(2,1)} %get-tuple-element.6.ig_in, bf16[384,1024]{1,0:T(8,128)(2,1)} %get-tuple-element.7.qg_in, bf16[2,256,256]{2,1,0:T(8,128)(2,1)} %get-tuple-element.8.wgt_in), custom_call_target="tpu_custom_call" | custom-call | tf_op jit(solution)/shard_map/finish/pallas_call | solution.py:610

commit v4 on v3

--- a/solution.py
+++ b/solution.py
@@ -8,6 +8,7 @@
 from jax.sharding import PartitionSpec as P
 
 HD = 128
+HEADS = 8
 BY_USE = (4, 3, 5, 2, 6, 1, 7, 0)
 MESH = pl.DeviceIdType.MESH
 F32 = jnp.float32
@@ -26,7 +27,7 @@
     li, q_in, k_in, v_in, w, do_in, dl,
     ig_out, qg_out, wg_out,
     q, k, v, do, probs, qg, xb, wz, wfull, kv_all, kv_oth, kvt, sbuf, rbuf, facc, xs, xr, fin, wgt,
-    iga, igo, igi, bias, kacc, vacc,
+    iga, igo, igi, pt, bias, kacc, vacc,
     in_sem, out_sem, xo_sem, xs_s, xs_r, xsib_s, xsib_r,
     w0_s, w0_r, wz_s, wz_r, wx_s, wx_r, wsib_s, wsib_r, wloc,
     k1_s, k1_r, k2_s, k2_r, ks_s, ks_r,
@@ -70,6 +71,58 @@
     for load in loads:
         load.start()
 
+    lens = [dl[0, i] for i in range(3)]
+    ends = [lens[0], lens[0] + lens[1], lens[0] + lens[1] + lens[2]]
+
+    def documents(shape, dim):
+        pos = lax.broadcasted_iota(jnp.int32, shape, dim)
+        return pos, sum((pos >= e).astype(jnp.int32) for e in ends)
+
+    kpos, kdoc = documents((384, 1), 0)
+    qpos, qdoc = documents((1, 384), 1)
+    bias[...] = jnp.where((kdoc == qdoc) & (kpos <= qpos), 0.0, -1e30).astype(F32)
+    scale = 1.0 / HD**0.5
+
+    def value_pass(b):
+        n = 128 * (b + 1)
+        rows = pl.ds(128 * b, 128)
+        total = None
+        for h in range(HEADS):
+            lanes = pl.ds(HD * h, HD)
+            s = dot(k[:n], q[rows, lanes], ((1,), (1,))) + bias[:n, 128 * b:n]
+            e = jnp.exp((s - jnp.max(s, axis=0, keepdims=True)) * scale)
+            soft = e * (1.0 / jnp.sum(e, axis=0, keepdims=True))
+            probs[h, :n, 128 * b:n] = soft
+            term = dot(soft.astype(BF16), do[rows, lanes], ((1,), (0,)))
+            total = term if total is None else total + term
+        add_rows(vacc, n, total)
+
+    def key_pass(b):
+        n = 128 * (b + 1)
+        rows = pl.ds(128 * b, 128)
+        total = None
+        for h in range(HEADS):
+            lanes = pl.ds(HD * h, HD)
+            soft = probs[h, :n, 128 * b:n]
+            pg = dot(v[:n], do[rows, lanes], ((1,), (1,)))
+            inner = jnp.sum(soft * pg, axis=0, keepdims=True)
+            ds = (soft * (pg - inner) * scale).astype(BF16)
+            qg[rows, lanes] = dot(ds, k[:n], ((0,), (0,))).astype(BF16)
+            term = dot(ds, q[rows, lanes], ((1,), (0,)))
+            total = term if total is None else total + term
+        add_rows(kacc, n, total)
+
+    def add_rows(acc, n, total):
+        if n == 384:
+            acc[...] = total
+        else:
+            acc[:n] += total
+
+    for load in loads:
+        load.wait()
+    for b in (2, 1, 0):
+        value_pass(b)
+
     pl.semaphore_wait(barrier, len(partners))
 
     rows_p = pl.ds(pl.multiple_of(p * 128, 128), 128)
@@ -112,13 +165,14 @@
     def block(dz):
         return (z + dz) % 8
 
-    for dz in BY_USE:
-        zp = block(dz)
-
-        @pl.when(zp // 4 == c)
-        def _():
-            for side in range(2):
-                x_send(side, zp).start()
+    def x_start(*dzs):
+        for dz in dzs:
+            zp = block(dz)
+
+            @pl.when(zp // 4 == c)
+            def _():
+                for side in range(2):
+                    x_send(side, zp).start()
 
     for dz in BY_USE:
         x_own(block(dz)).start()
@@ -201,45 +255,6 @@
         else:
             spread(arrived[0])
 
-    lens = [dl[0, i] for i in range(3)]
-    ends = [lens[0], lens[0] + lens[1], lens[0] + lens[1] + lens[2]]
-
-    def documents(shape, dim):
-        pos = lax.broadcasted_iota(jnp.int32, shape, dim)
-        return pos, sum((pos >= e).astype(jnp.int32) for e in ends)
-
-    kpos, kdoc = documents((384, 1), 0)
-    qpos, qdoc = documents((1, 384), 1)
-    bias[...] = jnp.where((kdoc == qdoc) & (kpos <= qpos), 0.0, -1e30).astype(F32)
-    kacc[...] = jnp.zeros_like(kacc)
-    vacc[...] = jnp.zeros_like(vacc)
-    scale = 1.0 / HD**0.5
-
-    def value_head(h, carry):
-        lanes = pl.ds(pl.multiple_of(h * HD, HD), HD)
-        for b in range(3):
-            n = 128 * (b + 1)
-            rows = pl.ds(128 * b, 128)
-            s = dot(k[:n], q[rows, lanes], ((1,), (1,))) + bias[:n, 128 * b:n]
-            e = jnp.exp((s - jnp.max(s, axis=0, keepdims=True)) * scale)
-            soft = e * (1.0 / jnp.sum(e, axis=0, keepdims=True))
-            probs[h, :n, 128 * b:n] = soft
-            vacc[:n] += dot(soft.astype(BF16), do[rows, lanes], ((1,), (0,)))
-        return carry
-
-    def key_head(h, carry):
-        lanes = pl.ds(pl.multiple_of(h * HD, HD), HD)
-        for b in range(3):
-            n = 128 * (b + 1)
-            rows = pl.ds(128 * b, 128)
-            soft = probs[h, :n, 128 * b:n]
-            pg = dot(v[:n], do[rows, lanes], ((1,), (1,)))
-            inner = jnp.sum(soft * pg, axis=0, keepdims=True)
-            ds = (soft * (pg - inner) * scale).astype(BF16)
-            qg[rows, lanes] = dot(ds, k[:n], ((0,), (0,))).astype(BF16)
-            kacc[:n] += dot(ds, q[rows, lanes], ((1,), (0,)))
-        return carry
-
     def part(i):
         return pl.ds(128 * (1 - i), 128)
 
@@ -287,10 +302,11 @@
         ref = (kv_all.at[core, yh], kv_all.at[core, 1 - yh], kv_oth.at[core])[i]
         return remote(ref, ref, ks_s.at[i], ks_r.at[i], sibling)
 
-    def partial(f, zp, first=0, count=128):
+    def bulk(f, *dzs):
         h = yh if f % 2 == 0 else 1 - yh
-        first += 128 * (1 - f // 2)
-        return dot(kvt[h, first:first + count, :], xb[zp], ((1,), (0,)))
+        first = 128 * (1 - f // 2)
+        for dz in dzs:
+            pt[f, dz] = dot(kvt[h, first:first + 128, :], xb[block(dz)], ((1,), (0,)))
 
     def rs_copy(f, direction, s):
         half = pl.ds(0, 64) if s == 0 else pl.ds(0, 128)
@@ -301,34 +317,28 @@
         )
 
     def rs_step(f, s):
-        terms = []
         for direction in range(2):
-            zd = (z + 4 - s) % 8 if direction == 0 else (z + 4 + s) % 8
+            dz = 4 - s if direction == 0 else 4 + s
             if s == 0:
-                terms.append(partial(f, zd, 64 * direction, 64))
-            else:
-                terms.append(partial(f, zd))
-        for direction in range(2):
-            term = terms[direction]
-            if s == 0:
-                sbuf[f, direction, 0, :64] = term.astype(BF16)
+                mine = slice(64 * direction, 64 * direction + 64)
+                sbuf[f, direction, 0, :64] = pt[f, 4, mine].astype(BF16)
             else:
                 rs_copy(f, direction, s - 1).wait_recv()
                 if s == 1:
                     mine = slice(64 * direction, 64 * direction + 64)
                     rest = slice(64 - 64 * direction, 128 - 64 * direction)
-                    sbuf[f, direction, 1, rest] = term[rest].astype(BF16)
+                    sbuf[f, direction, 1, rest] = pt[f, dz, rest].astype(BF16)
                     sbuf[f, direction, 1, mine] = (
-                        term[mine] + rbuf[f, direction, 0, :64].astype(F32)
+                        pt[f, dz, mine] + rbuf[f, direction, 0, :64].astype(F32)
                     ).astype(BF16)
                 else:
                     sbuf[f, direction, s] = (
-                        term + rbuf[f, direction, s - 1].astype(F32)
+                        pt[f, dz] + rbuf[f, direction, s - 1].astype(F32)
                     ).astype(BF16)
             rs_copy(f, direction, s).start()
 
     def rs_last(f):
-        total = partial(f, z)
+        total = pt[f, 0]
         for direction in range(2):
             rs_copy(f, direction, 3).wait_recv()
             total = total + rbuf[f, direction, 3].astype(F32)
@@ -381,20 +391,23 @@
             igo.at[j], igi.at[j], ig_s.at[j], ig_r.at[j], device(x, 2 * yh + 1 - yl, z, c)
         )
 
-    def ig_step(j):
+    def rows_of(kv, j):
+        total = None
+        for cc in range(2):
+            for h in range(2):
+                term = dot(kv[cc, h], wfull[j, cc, h], ((1,), (1,)))
+                total = term if total is None else total + term
+        return total.astype(BF16)
+
+    def ig_other(r):
+        j = (z + r) % 4
         w_ready(j)
-
-        def rows_of(kv):
-            total = None
-            for cc in range(2):
-                for h in range(2):
-                    term = dot(kv[cc, h], wfull[j, cc, h], ((1,), (1,)))
-                    total = term if total is None else total + term
-            return total.astype(BF16)
-
-        igo[j] = rows_of(kv_oth)
+        igo[j] = rows_of(kv_oth, j)
         ig_copy(j).start()
-        iga[j] = rows_of(kv_all)
+
+    def ig_own(r):
+        j = (z + r) % 4
+        iga[j] = rows_of(kv_all, j)
         ig_store(j, 0).start()
 
     def ig_store(j, other):
@@ -403,80 +416,97 @@
         src = iga.at[j] if other == 0 else igi.at[j]
         return pltpu.make_async_copy(src, ig_out.at[:, cols], out_sem.at[2 * j + other])
 
-    def ig_last(j):
+    def ig_last(r):
+        j = (z + r) % 4
         ig_copy(j).wait_recv()
         ig_store(j, 1).start()
 
     qg_store = pltpu.make_async_copy(qg, qg_out, out_sem.at[8])
     wg_store = pltpu.make_async_copy(wgt, wg_out, out_sem.at[9])
 
-    for load in loads:
-        load.wait()
-    lax.fori_loop(0, 2, value_head, 0)
+    kv1_start(0, vacc)
+    x_start(4, 3, 5)
+    key_pass(2)
     w_begin()
-    lax.fori_loop(2, 8, value_head, 0)
-    kv1_start(0, vacc)
-    lax.fori_loop(0, 2, key_head, 0)
-    for dz in BY_USE[:3]:
-        x_pass(dz)
-    w_step(0)
-    lax.fori_loop(2, 5, key_head, 0)
-    kv1_ready(0)
-    x_ready(4)
-    rs_step(0, 0)
-    lax.fori_loop(5, 8, key_head, 0)
+    key_pass(1)
+    key_pass(0)
     kv1_start(1, kacc)
     qg_store.start()
+    kv1_ready(0)
+    x_start(2, 6, 1, 7, 0)
     kv_sibling(0, c).start()
-    for dz in BY_USE[3:]:
-        x_pass(dz)
-    w_step(1)
+    x_pass(4)
+    x_pass(3)
+    x_pass(5)
+    w_step(0)
+    x_ready(4)
+    bulk(0, 4)
+    rs_step(0, 0)
+    kv2_ready(0)
+    bulk(1, 4)
+    rs_step(1, 0)
     x_ready(3)
     x_ready(5)
+    bulk(0, 3, 5)
     rs_step(0, 1)
-    kv2_ready(0)
-    rs_step(1, 0)
+    bulk(1, 3, 5)
     kv1_ready(1)
     kv_sibling(2, c).start()
+    w_step(1)
+    bulk(2, 4, 3, 5)
     rs_step(2, 0)
+    rs_step(1, 1)
+    x_pass(2)
+    x_pass(6)
+    kv2_ready(1)
+    kv_sibling(1, c).start()
+    bulk(3, 4, 3, 5)
+    rs_step(3, 0)
+    x_pass(1)
+    x_pass(7)
+    x_pass(0)
+    w_step(2)
     x_ready(2)
     x_ready(6)
-    w_step(2)
+    for f in range(4):
+        bulk(f, 2, 6)
     rs_step(0, 2)
-    rs_step(1, 1)
-    kv2_ready(1)
-    kv_sibling(1, c).start()
-    rs_step(3, 0)
     rs_step(2, 1)
-    x_ready(1)
-    x_ready(7)
+    kv_sibling(2, 1 - c).wait_recv()
+    ig_other(1)
+    rs_step(1, 2)
+    ig_other(2)
+    rs_step(3, 1)
+    for dz in (1, 7, 0):
+        x_ready(dz)
+    for f in range(4):
+        bulk(f, 1, 7, 0)
     rs_step(0, 3)
+    ig_other(3)
     w_step(3)
-    rs_step(1, 2)
-    rs_step(3, 1)
     rs_step(2, 2)
-    x_ready(0)
+    rs_step(1, 3)
     rs_last(0)
-    for i in range(3):
-        kv_sibling(i, 1 - c).wait_recv()
-    ig_step(0)
-    rs_step(1, 3)
     rs_step(3, 2)
-    ig_step(1)
+    ig_other(0)
     rs_step(2, 3)
     rs_last(1)
     x_first(0)
-    ig_step(2)
     rs_step(3, 3)
+    for i in range(2):
+        kv_sibling(i, 1 - c).wait_recv()
+    ig_own(0)
     rs_last(2)
-    ig_step(3)
+    ig_own(1)
     x_last(0)
     rs_last(3)
     x_first(1)
-    for j in range(3):
-        ig_last(j)
+    ig_own(2)
+    ig_own(3)
+    for r in (1, 2, 3):
+        ig_last(r)
     x_last(1)
-    ig_last(3)
+    ig_last(0)
 
     for i in range(2):
         for hs in range(2):
@@ -589,6 +619,7 @@
             pltpu.VMEM((4, 384, 256), BF16),
             pltpu.VMEM((4, 384, 256), BF16),
             pltpu.VMEM((4, 384, 256), BF16),
+            pltpu.VMEM((4, 8, 128, 256), F32),
             pltpu.VMEM((384, 384), F32),
             pltpu.VMEM((384, 128), F32),
             pltpu.VMEM((384, 128), F32),

time: 71.3 us -> 65 us (0.912)
  Pallas kernels: 70.5 us -> 63.9 us
    pallas_call x1, Pallas kernels: 67.8 us -> 61.1 us  [shards(): pl.pallas_call(kernel, out_shape=(jax.ShapeDtypeStruct((384, 2048), BF16)...]
where the time goes in v4:
time: 65 us; the launch traced here: 64.6 us
  Pallas kernels  63.9 us (98%)
    pallas_call x1, Pallas kernels, shards(): pl.pallas_call(kernel, out_shape=(jax.ShapeDtypeStruct((384, 2048), BF16)...  61.1 us
    pallas_call x1, Pallas kernels, shards(): pl.pallas_call(finish, out_shape=(jax.ShapeDtypeStruct((384, 2048), BF16)...  2.78 us

profile of v4, /device:TPU:2, one launch (start us, length us, event | category | flops | bytes accessed | tf_op | source)
XLA Modules:
  0.0 64.6 jit_solution(14130246112996357669)
XLA Ops:
  0.6 61.1 %kv_back.1 = (bf16[384,2048]{1,0:T(8,128)(2,1)}, bf16[384,1024]{1,0:T(8,128)(2,1)}, bf16[2,256,256]{2,1,0:T(8,128)(2,1)}) custom-call(bf16[384,8192]{1,0:T(8,128)(2,1)} %li.1, bf16[384,1024]{1,0:T(8,128)(2,1)} %q_in.1, bf16[384,128]{1,0:T(8,128)(2,1)} %k_in.1, bf16[384,128]{1,0:T(8,128)(2,1)} %v_in.1, bf16[512,256]{1,0:T(8,128)(2,1)} %w.1, ...), custom_call_target="tpu_custom_call" | custom-call | flops 5000000000 | bytes 20000000 | tf_op jit(solution)/shard_map/kv_back/pallas_call | solution.py:590
  61.8 2.8 %finish.1 = (bf16[384,2048]{1,0:T(8,128)(2,1)}, bf16[384,1024]{1,0:T(8,128)(2,1)}, f32[512,256]{1,0:T(8,128)}) custom-call(bf16[384,2048]{1,0:T(8,128)(2,1)} %get-tuple-element.6.ig_in, bf16[384,1024]{1,0:T(8,128)(2,1)} %get-tuple-element.7.qg_in, bf16[2,256,256]{2,1,0:T(8,128)(2,1)} %get-tuple-element.8.wgt_in), custom_call_target="tpu_custom_call" | custom-call | tf_op jit(solution)/shard_map/finish/pallas_call | solution.py:641

commit v5 on v4

--- a/solution.py
+++ b/solution.py
@@ -433,7 +433,7 @@
     kv1_start(1, kacc)
     qg_store.start()
     kv1_ready(0)
-    x_start(2, 6, 1, 7, 0)
+    x_start(2, 6)
     kv_sibling(0, c).start()
     x_pass(4)
     x_pass(3)
@@ -443,6 +443,7 @@
     bulk(0, 4)
     rs_step(0, 0)
     kv2_ready(0)
+    x_start(1, 7, 0)
     bulk(1, 4)
     rs_step(1, 0)
     x_ready(3)
@@ -472,11 +473,11 @@
         bulk(f, 2, 6)
     rs_step(0, 2)
     rs_step(2, 1)
+    rs_step(1, 2)
     kv_sibling(2, 1 - c).wait_recv()
-    ig_other(1)
-    rs_step(1, 2)
     ig_other(2)
     rs_step(3, 1)
+    ig_other(1)
     for dz in (1, 7, 0):
         x_ready(dz)
     for f in range(4):
@@ -503,19 +504,10 @@
     x_first(1)
     ig_own(2)
     ig_own(3)
-    for r in (1, 2, 3):
+    for r in (2, 1, 3):
         ig_last(r)
     x_last(1)
     ig_last(0)
-
-    for i in range(2):
-        for hs in range(2):
-            for xx in range(4):
-                cols = pl.ds(128 * (1 - i) + 32 * xx, 32)
-                remote(
-                    fin.at[0, 0], wgt.at[hs, cols], fin_s.at[0, 0, 0], fin_r.at[i, hs, xx], sibling
-                ).wait_recv()
-    wg_store.start()
 
     for i in range(2):
         @pl.when(2 * yl + i != y)
@@ -549,10 +541,20 @@
     for i in range(2):
         for n in range(1, 4):
             x_copy(i, n).wait_send()
+    qg_store.wait()
+
+    for i in range(2):
+        for hs in range(2):
+            for xx in range(4):
+                cols = pl.ds(128 * (1 - i) + 32 * xx, 32)
+                remote(
+                    fin.at[0, 0], wgt.at[hs, cols], fin_s.at[0, 0, 0], fin_r.at[i, hs, xx], sibling
+                ).wait_recv()
+    wg_store.start()
+    for i in range(2):
         for slot in range(2):
             for n in range(4):
                 fin_copy(i, slot, n).wait_send()
-    qg_store.wait()
     wg_store.wait()
 
 

time: 65 us -> 65.1 us (level)
  no operation moved by 1% of the time
where the time goes in v5:
time: 65.1 us; the launch traced here: 65 us
  Pallas kernels  64.3 us (99%)
    pallas_call x1, Pallas kernels, shards(): pl.pallas_call(kernel, out_shape=(jax.ShapeDtypeStruct((384, 2048), BF16)...  61.6 us
    pallas_call x1, Pallas kernels, shards(): pl.pallas_call(finish, out_shape=(jax.ShapeDtypeStruct((384, 2048), BF16)...  2.78 us

profile of v5, /device:TPU:2, one launch (start us, length us, event | category | flops | bytes accessed | tf_op | source)
XLA Modules:
  0.0 65.0 jit_solution(1530325865391824588)
XLA Ops:
  0.6 61.6 %kv_back.1 = (bf16[384,2048]{1,0:T(8,128)(2,1)}, bf16[384,1024]{1,0:T(8,128)(2,1)}, bf16[2,256,256]{2,1,0:T(8,128)(2,1)}) custom-call(bf16[384,8192]{1,0:T(8,128)(2,1)} %li.1, bf16[384,1024]{1,0:T(8,128)(2,1)} %q_in.1, bf16[384,128]{1,0:T(8,128)(2,1)} %k_in.1, bf16[384,128]{1,0:T(8,128)(2,1)} %v_in.1, bf16[512,256]{1,0:T(8,128)(2,1)} %w.1, ...), custom_call_target="tpu_custom_call" | custom-call | flops 5000000000 | bytes 20000000 | tf_op jit(solution)/shard_map/kv_back/pallas_call | solution.py:592
  62.2 2.8 %finish.1 = (bf16[384,2048]{1,0:T(8,128)(2,1)}, bf16[384,1024]{1,0:T(8,128)(2,1)}, f32[512,256]{1,0:T(8,128)}) custom-call(bf16[384,2048]{1,0:T(8,128)(2,1)} %get-tuple-element.6.ig_in, bf16[384,1024]{1,0:T(8,128)(2,1)} %get-tuple-element.7.qg_in, bf16[2,256,256]{2,1,0:T(8,128)(2,1)} %get-tuple-element.8.wgt_in), custom_call_target="tpu_custom_call" | custom-call | tf_op jit(solution)/shard_map/finish/pallas_call | solution.py:643
